TPU v7x, 32 devices: a whole 2x2x4 slice. The times are simulated.
32 devices in a mesh: groups: 2 (over x), ep: 16 (over z, y, core).
Axes of the slice: x: 2, y: 2, z: 4, core: 2. Of those that a mesh axis runs over, the one named last changes fastest.
Arguments:
- inputs: float32 [64, 6144], P(('groups', 'ep')), parts along dimension 0, may hold values from -6 to 6
- norm_gain: float32 [6144], replicated, may hold values from 0.5 to 1.5
- dense_gate: bfloat16 [6144, 12288], P(None, 'ep'), may hold values from -0.078125 to 0.078125
- dense_up: bfloat16 [6144, 12288], P(None, 'ep'), may hold values from -0.078125 to 0.078125
- dense_down: bfloat16 [12288, 6144], P('ep'), may hold values from -0.0546875 to 0.0546875
- expert_gate: bfloat16 [6144, 32768], P(None, 'ep'), may hold values from -0.078125 to 0.078125
- expert_up: bfloat16 [6144, 32768], P(None, 'ep'), may hold values from -0.078125 to 0.078125
- expert_down: bfloat16 [32768, 6144], P('ep'), may hold values from -0.125 to 0.125
- expert_ids: int32 [64, 12], P('groups'), parts along dimension 0, may hold values from 0 to 16, all different within a row; in each aligned block of 2 rows (0 to 1, 2 to 3, ...) at most 2 rows name the same one
- route_weights: int32 [64, 12], P('groups'), parts along dimension 0, may hold values from 1 to 1024
- out_gain: float32 [6144], replicated, may hold values from 0.5 to 1.5
Outputs:
- result: float32 [64, 6144], P(('groups', 'ep')), parts along dimension 0
There are 2 independent parts, one for each index of `groups`. A program takes and returns all parts, laid end to end along the dimension named above; an argument that names none is the same for every part. Nothing has to cross between parts.
Inputs may be any that keep to these rules, and one draw needn't show every extreme that they name: `expert_ids`: each row names 12 different values; in the rows of one device (aligned blocks of 2 rows) no value is named by more than 2 rows, and in every draw some value is named by exactly 2 rows of one device.
All inputs are finite; a program needn't handle non-finite values.
Results may differ from a plain program's by a relative error of at most 0.0031.
Values may be sent and summed in bfloat16 or wider, within the bound.
No kernel may reach another device: no remote copies, remote signals or barrier semaphores. Data moves between devices by JAX's collectives and lax.ppermute only.
A program may use at most 192 MiB of HBM per device.

v0:
```python
import jax
import jax.numpy as jnp
from jax import lax
from jax.sharding import PartitionSpec as P

EXPERTS = 16
MOST = 2


def rms_scale(values):
    return values * lax.rsqrt(jnp.mean(values * values, axis=-1, keepdims=True) + 1e-06)


def slot_table(expert_ids, weights_all, expert, blocks, block_rows):
    matches = expert_ids == expert
    picked = jnp.any(matches, axis=1).reshape(blocks, block_rows)
    weight = jnp.sum(jnp.where(matches, weights_all, 0.0), axis=1).reshape(blocks, block_rows)
    ranking = jnp.cumsum(picked.astype(jnp.int32), axis=1) - 1
    position = lax.broadcasted_iota(jnp.int32, (blocks, block_rows), 1)
    row_cols = []
    weight_cols = []
    for column in range(MOST):
        chosen = picked & (ranking == column)
        row_cols.append(jnp.sum(jnp.where(chosen, position, 0), axis=1))
        weight_cols.append(jnp.sum(jnp.where(chosen, weight, 0.0), axis=1))
    offsets = lax.broadcasted_iota(jnp.int32, (blocks, 1), 0) * block_rows
    slot_rows = (jnp.stack(row_cols, axis=1) + offsets).reshape(-1)
    slot_weight = jnp.stack(weight_cols, axis=1).reshape(-1)
    return (slot_rows, slot_weight)


def on_device(
    inputs,
    norm_gain,
    dense_gate,
    dense_up,
    dense_down,
    expert_gate,
    expert_up,
    expert_down,
    expert_ids,
    route_weights,
    out_gain,
):
    devices = lax.axis_size("ep")
    rows_own = inputs.shape[0]
    width = inputs.shape[1]
    slices = devices // EXPERTS
    my_index = lax.axis_index("ep")
    expert = my_index // slices
    hidden_in = (rms_scale(inputs) * norm_gain).astype(jnp.bfloat16)
    gathered = lax.all_gather(hidden_in, "ep", axis=0, tiled=True)
    gate = jnp.dot(gathered, dense_gate, preferred_element_type=jnp.float32)
    upper = jnp.dot(gathered, dense_up, preferred_element_type=jnp.float32)
    dense_hidden = (jax.nn.silu(gate) * upper).astype(jnp.bfloat16)
    weights_all = route_weights.astype(jnp.float32) / 1024.0
    slot_rows, slot_weight = slot_table(expert_ids, weights_all, expert, devices, rows_own)
    picked_in = gathered[slot_rows]
    e_gate = jnp.dot(picked_in, expert_gate, preferred_element_type=jnp.float32)
    e_upper = jnp.dot(picked_in, expert_up, preferred_element_type=jnp.float32)
    e_hidden = (jax.nn.silu(e_gate) * e_upper).astype(jnp.bfloat16)
    partial_value = (
        jnp.dot(e_hidden, expert_down, preferred_element_type=jnp.float32) * slot_weight[:, None]
    )
    own_start = my_index * rows_own
    own_ids = lax.dynamic_slice_in_dim(expert_ids, own_start, rows_own, 0)
    own_weights = lax.dynamic_slice_in_dim(weights_all, own_start, rows_own, 0)
    zero_weight = jnp.sum(jnp.where(own_ids == EXPERTS, own_weights, 0.0), axis=1)
    local_moe = zero_weight[:, None] * hidden_in.astype(jnp.float32)
    spread = jnp.zeros((gathered.shape[0], width), jnp.float32).at[slot_rows].add(partial_value)
    summed = lax.psum_scatter(
        jnp.dot(dense_hidden, dense_down, preferred_element_type=jnp.float32) + spread,
        "ep",
        scatter_dimension=0,
        tiled=True,
    )
    joined = summed + local_moe
    return inputs + rms_scale(joined) * out_gain


def solution(mesh):
    placed = (
        P(("groups", "ep"), None),
        P(),
        P(None, "ep"),
        P(None, "ep"),
        P("ep", None),
        P(None, "ep"),
        P(None, "ep"),
        P("ep", None),
        P("groups", None),
        P("groups", None),
        P(),
    )
    return jax.shard_map(
        on_device, mesh=mesh, in_specs=placed, out_specs=P(("groups", "ep"), None), check_vma=False
    )
```

profile of v0, /device:TPU:0, one launch (start us, length us, event | category | flops | bytes accessed | tf_op | source)
XLA Modules:
  0.0 182.3 jit_solution(16079961452170177742)
XLA Ops:
  6.5 1.0 multiply_reduce_fusion.1
  7.5 0.9 fusion.30
  8.4 24.2 %all-gather = bf16[16,2,6144]{2,1,0:T(2,128)(2,1)S(1)} all-gather(bf16[1,2,6144]{2,1,0:T(2,128)(2,1)S(1)} %fusion.30), channel_id=1, replica_groups=mesh['groups'=2,'ep'=16] {'ep'}, dimensions={0}, use_global_device_ids=true | all-gather | bytes 417792 | tf_op jit(solution)/shard_map/all_gather | solution.py:52
  32.6 0.1 reshape.80
  32.8 0.7 select_reduce_fusion.3
  33.6 0.1 reshape.61
  33.7 0.2 reduce_window_sum.11
  33.9 0.1 select_reduce_fusion.2
  34.0 0.1 select_reduce_fusion.4
  34.1 0.1 copy.16
  34.2 0.1 add.76
  34.3 5.3 %fusion.18 = f32[32,768]{1,0:T(8,128)S(1)} fusion(bf16[32,6144]{1,0:T(8,128)(2,1)S(1)} %reshape.80, bf16[6144,768]{1,0:T(8,128)(2,1)} %param.13), kind=kOutput, calls=%fused_computation.46 | convolution fusion | flops 301989888 | bytes 9928704 | tf_op jit(solution)/shard_map/dot_general | solution.py:53
  39.7 0.8 gather_fusion
  40.6 0.1 mul.91
  40.7 10.4 %fusion.19 = f32[32,2048]{1,0:T(8,128)S(1)} fusion(bf16[32,6144]{1,0:T(8,128)(2,1)S(1)} %gather_fusion, bf16[6144,2048]{1,0:T(8,128)(2,1)} %param.16), kind=kOutput, calls=%fused_computation.47 | convolution fusion | flops 805306368 | bytes 25821184 | tf_op jit(solution)/shard_map/dot_general | solution.py:59
  51.1 10.2 %fusion.2 = f32[32,6144]{1,0:T(8,128)S(1)} fusion(bf16[768,6144]{1,0:T(8,128)(2,1)} %param.15, bf16[32,6144]{1,0:T(8,128)(2,1)S(1)} %reshape.80, bf16[6144,768]{1,0:T(8,128)(2,1)} %param.14, f32[32,768]{1,0:T(8,128)S(1)} %fusion.18), kind=kOutput, calls=%fused_computation.7 | convolution fusion | flops 604127232 | bytes 20152320 | tf_op jit(solution)/shard_map/dot_general | solution.py:72
  61.3 19.9 %convolution_multiply_fusion = f32[32,6144]{1,0:T(8,128)S(1)} fusion(bf16[2048,6144]{1,0:T(8,128)(2,1)} %param.18, bf16[32,6144]{1,0:T(8,128)(2,1)S(1)} %gather_fusion, bf16[6144,2048]{1,0:T(8,128)(2,1)} %param.17, f32[32]{0:T(128)S(1)} %mul.91, f32[32,2048]{1,0:T(8,128)S(1)} %fusion.19), kind=kOutput, calls=%fused_computation.2 | convolution fusion | flops 1611202560 | bytes 51773568 | tf_op jit(solution)/shard_map/dot_general | solution.py:63
  81.2 1.8 scatter_fusion
  83.0 0.9 copy-done
  84.0 0.6 dynamic-slice
  85.2 0.1 select_reduce_fusion
  85.3 88.2 %all-reduce.3.cloned.1.call-done = f32[32,6144]{1,0:T(8,128)} async-done(((f32[32,6144]{1,0:T(8,128)}), f32[32,6144]{1,0:T(8,128)}) %all-reduce.3.cloned.1.call-update) | async-done | bytes 786448
  173.5 1.2 multiply_reduce_fusion
  174.7 0.7 multiply_add_fusion
  (24 shorter events, 0.3 us)
Async XLA Ops:
  6.5 167.0 %all-reduce.3.cloned.1.call-start = ((), (), s32[]{:S(2)}) async-start(), calls=%async_computation | async-start | bytes 1572864
  61.2 22.7 %copy-start.5 = (u32[32]{0:T(128)S(1)}, u32[32]{0:T(128)}, u32[]{:S(2)}) copy-start(u32[32]{0:T(128)} %constant.56) | copy-start | bytes 388
  61.2 24.0 %copy-start.3 = (s32[32,12]{0,1:T(8,128)S(1)}, s32[32,12]{0,1:T(8,128)}, u32[]{:S(2)}) copy-start(s32[32,12]{0,1:T(8,128)} %param.19) | copy-start | bytes 4612
  61.3 112.3 %copy-start.1 = (f32[2,6144]{1,0:T(2,128)S(1)}, f32[2,6144]{1,0:T(2,128)}, u32[]{:S(2)}) copy-start(f32[2,6144]{1,0:T(2,128)} %param.11) | copy-start | bytes 147460
  61.3 112.3 %copy-start.2 = (f32[6144]{0:T(1024)S(1)}, f32[6144]{0:T(1024)}, u32[]{:S(2)}) copy-start(f32[6144]{0:T(1024)} %param.12) | copy-start | bytes 73732
  61.3 113.4 %copy-start.4 = (f32[6144]{0:T(1024)S(1)}, f32[6144]{0:T(1024)}, u32[]{:S(2)}) copy-start(f32[6144]{0:T(1024)} %param.21) | copy-start | bytes 73732
  83.0 0.9 copy-start
Sparse Core Ops, SparseCore 0:
  84.1 89.4 all-reduce.2
where the time goes:
time: 183 us; the launch traced here: 182 us
  waiting for transfers between devices  88.2 us (48%)
  matrix products  45.8 us (25%)
  blocking collectives  24.2 us (13%)
  between operations  14.2 us (8%)
  other arithmetic  6.89 us (4%)
  local copies, waits for them, and re-layouts  2.98 us (2%)
    unnamed x2, waiting for transfers between devices  88.2 us
    all_gather x1, blocking collectives, on_device(): gathered = lax.all_gather(hidden_in, 'ep', axis=0, tiled=True)  24.2 us
    dot_general x1, matrix products, on_device(): jnp.dot(e_hidden, expert_down, preferred_element_type=jnp.float32)  19.9 us
    dot_general x1, matrix products, on_device(): e_gate = jnp.dot(picked_in, expert_gate, preferred_element_type=jnp.float32)  10.4 us
    dot_general x1, matrix products, on_device(): jnp.dot(dense_hidden, dense_down, preferred_element_type=jnp.float32)  10.2 us
    dot_general x1, matrix products, on_device(): gate = jnp.dot(gathered, dense_gate, preferred_element_type=jnp.float32)  5.33 us
  transfers between devices with their start and end apart: 1, of which 1 were waited for; matrix products, arithmetic and copies ran while one was open for 0% of the time, Pallas kernels for 0%

commit v1 on v0

v1 whole, which is shorter than its diff:
```python
import functools

import jax
import jax.numpy as jnp
from jax import lax
from jax.experimental import pallas as pl
from jax.experimental.pallas import tpu as pltpu
from jax.sharding import PartitionSpec as P

EXPERTS = 16
BF16, F32 = jnp.bfloat16, jnp.float32
VMEM = pl.BlockSpec(memory_space=pltpu.VMEM)
SMEM = pl.BlockSpec(memory_space=pltpu.SMEM)
HBM = pl.BlockSpec(memory_space=pl.ANY)


def in_hbm(array):
    return pltpu.with_memory_space_constraint(array, pltpu.HBM)


def in_vmem(array):
    return pltpu.with_memory_space_constraint(array, pltpu.VMEM)


def block_of(extent, most):
    fits = [b for b in range(128, min(most, extent) + 1, 128) if extent % b == 0]
    return fits[-1] if fits else extent


def rms_scale(values):
    return values * lax.rsqrt(jnp.mean(values * values, axis=-1, keepdims=True) + 1e-06)


def norm_rows(inputs_ref, gain_ref, out_ref):
    out_ref[...] = (rms_scale(inputs_ref[...]) * gain_ref[...]).astype(out_ref.dtype)


def normed(inputs, gain):
    return pl.pallas_call(
        norm_rows,
        out_shape=jax.ShapeDtypeStruct(inputs.shape, BF16),
        in_specs=[VMEM, VMEM],
        out_specs=VMEM,
        compiler_params=pltpu.CompilerParams(vmem_limit_bytes=8 << 20),
    )(inputs, gain.reshape(1, -1))


class Stream:
    def __init__(self, sources, slots, sems, steps, at):
        self.sources, self.slots, self.sems, self.steps, self.at = sources, slots, sems, steps, at
        self.depth = slots[0].shape[0]

    def copies(self, step, slot):
        return [
            pltpu.make_async_copy(self.at(source, step), buffer.at[slot], self.sems.at[i, slot])
            for i, (source, buffer) in enumerate(zip(self.sources, self.slots))
        ]

    def fill(self):
        for step in range(min(self.depth, self.steps)):
            for copy in self.copies(step, step):
                copy.start()

    def run(self, use):
        def body(step, _):
            slot = lax.rem(step, self.depth)
            for copy in self.copies(step, slot):
                copy.wait()
            use(step, [buffer.at[slot] for buffer in self.slots])

            @pl.when(step + self.depth < self.steps)
            def _():
                for copy in self.copies(step + self.depth, slot):
                    copy.start()

            return 0

        lax.fori_loop(0, self.steps, body, 0)


def aligned(step, size):
    return pl.ds(pl.multiple_of(step * size, size), size)


def column_weights(expert, ids_ref, route_ref):
    count = ids_ref.shape[1]
    across = jnp.sum(
        jnp.where(ids_ref[...] == expert, route_ref[...].astype(F32) / 1024.0, 0.0),
        axis=0,
        keepdims=True,
    )
    same = lax.broadcasted_iota(jnp.int32, (count, count), 0) == lax.broadcasted_iota(
        jnp.int32, (count, count), 1
    )
    return jnp.sum(jnp.where(same, across, 0.0), axis=1, keepdims=True)


def branches(
    expert_ref,
    rows_ref,
    ids_ref,
    route_ref,
    eg_ref,
    eu_ref,
    dg_ref,
    du_ref,
    dd_ref,
    ed_ref,
    out_ref,
    eg_slots,
    eu_slots,
    dg_slots,
    du_slots,
    dd_slots,
    ed_slots,
    eg_sum,
    eu_sum,
    dg_sum,
    du_sum,
    first_sems,
    second_sems,
):
    width = rows_ref.shape[1]
    kb, cb = eg_slots.shape[1], dd_slots.shape[2]
    first = Stream(
        [eg_ref, eu_ref, dg_ref, du_ref],
        [eg_slots, eu_slots, dg_slots, du_slots],
        first_sems,
        width // kb,
        lambda ref, step: ref.at[aligned(step, kb), :],
    )
    second = Stream(
        [dd_ref, ed_ref],
        [dd_slots, ed_slots],
        second_sems,
        width // cb,
        lambda ref, step: ref.at[:, aligned(step, cb)],
    )
    first.fill()
    second.fill()
    sums = [eg_sum, eu_sum, dg_sum, du_sum]
    for total in sums:
        total[...] = jnp.zeros_like(total)

    def gate_up(step, blocks):
        part = rows_ref[:, aligned(step, kb)]
        for total, block in zip(sums, blocks):
            total[...] += jnp.dot(part, block[...], preferred_element_type=F32)

    first.run(gate_up)
    e_hidden = (jax.nn.silu(eg_sum[...]) * eu_sum[...]).astype(BF16)
    d_hidden = (jax.nn.silu(dg_sum[...]) * du_sum[...]).astype(BF16)
    weight = column_weights(expert_ref[0], ids_ref, route_ref)

    def down(step, blocks):
        dense = jnp.dot(d_hidden, blocks[0][...], preferred_element_type=F32)
        routed = jnp.dot(e_hidden, blocks[1][...], preferred_element_type=F32)
        out_ref[:, aligned(step, cb)] = (dense + routed * weight).astype(out_ref.dtype)

    second.run(down)


def branch_sums(expert, rows, ids, route, e_gate, e_up, d_gate, d_up, d_down, e_down):
    count, width = rows.shape
    dense, units = d_gate.shape[1], e_gate.shape[1]
    kb, cb = block_of(width, 256), block_of(width, 512)
    depth = 3
    weights = [in_hbm(a) for a in (e_gate, e_up, d_gate, d_up, d_down, e_down)]
    return pl.pallas_call(
        branches,
        out_shape=jax.ShapeDtypeStruct((count, width), BF16),
        in_specs=[SMEM, VMEM, VMEM, VMEM] + [HBM] * 6,
        out_specs=VMEM,
        scratch_shapes=[
            pltpu.VMEM((depth, kb, units), BF16),
            pltpu.VMEM((depth, kb, units), BF16),
            pltpu.VMEM((depth, kb, dense), BF16),
            pltpu.VMEM((depth, kb, dense), BF16),
            pltpu.VMEM((depth, dense, cb), BF16),
            pltpu.VMEM((depth, units, cb), BF16),
            pltpu.VMEM((count, units), F32),
            pltpu.VMEM((count, units), F32),
            pltpu.VMEM((count, dense), F32),
            pltpu.VMEM((count, dense), F32),
            pltpu.SemaphoreType.DMA((4, depth)),
            pltpu.SemaphoreType.DMA((2, depth)),
        ],
        compiler_params=pltpu.CompilerParams(vmem_limit_bytes=40 << 20),
        cost_estimate=pl.CostEstimate(
            flops=6 * count * width * (dense + units),
            bytes_accessed=6 * width * (dense + units),
            transcendentals=count * (dense + units),
        ),
    )(expert, rows, ids, route, *weights)


def join(
    first_ref, received_ref, hidden_ref, ids_ref, route_ref, inputs_ref, gain_ref, out_ref
):
    rows = inputs_ref.shape[0]
    summed = jnp.sum(received_ref[...].astype(F32), axis=0)
    count = ids_ref.shape[1]
    across = jnp.sum(
        jnp.where(ids_ref[...] == EXPERTS, route_ref[...].astype(F32) / 1024.0, 0.0),
        axis=0,
        keepdims=True,
    )
    mine = lax.broadcasted_iota(jnp.int32, (rows, count), 1) == first_ref[
        0
    ] + lax.broadcasted_iota(jnp.int32, (rows, count), 0)
    zero_weight = jnp.sum(jnp.where(mine, across, 0.0), axis=1, keepdims=True)
    joined = summed + zero_weight * hidden_ref[...].astype(F32)
    out_ref[...] = inputs_ref[...] + rms_scale(joined) * gain_ref[...]


def joined_rows(first, received, hidden, ids, route, inputs, gain):
    return pl.pallas_call(
        join,
        out_shape=jax.ShapeDtypeStruct(inputs.shape, F32),
        in_specs=[SMEM] + [VMEM] * 6,
        out_specs=VMEM,
        compiler_params=pltpu.CompilerParams(vmem_limit_bytes=24 << 20),
    )(first, in_vmem(received), hidden, ids, route, inputs, gain.reshape(1, -1))


def on_device(
    inputs,
    norm_gain,
    dense_gate,
    dense_up,
    dense_down,
    expert_gate,
    expert_up,
    expert_down,
    expert_ids,
    route_weights,
    out_gain,
):
    devices = lax.axis_size("ep")
    rows_own, width = inputs.shape
    my_index = lax.axis_index("ep")
    expert = my_index // (devices // EXPERTS)
    ids, route = expert_ids.T, route_weights.T
    hidden_in = normed(inputs, norm_gain)
    gathered = lax.all_gather(hidden_in, "ep", axis=0, tiled=True)
    partial = branch_sums(
        expert[None],
        gathered,
        ids,
        route,
        expert_gate,
        expert_up,
        dense_gate,
        dense_up,
        dense_down,
        expert_down,
    )
    received = lax.all_to_all(
        partial.reshape(devices, rows_own, width), "ep", 0, 0, tiled=True
    )
    return joined_rows(
        (my_index * rows_own)[None], received, hidden_in, ids, route, inputs, out_gain
    )


def solution(mesh):
    placed = (
        P(("groups", "ep"), None),
        P(),
        P(None, "ep"),
        P(None, "ep"),
        P("ep", None),
        P(None, "ep"),
        P(None, "ep"),
        P("ep", None),
        P("groups", None),
        P("groups", None),
        P(),
    )
    return jax.shard_map(
        on_device, mesh=mesh, in_specs=placed, out_specs=P(("groups", "ep"), None), check_vma=False
    )
```

time: 183 us -> 80.1 us (0.44)
  waiting for transfers between devices: 88.2 us -> 12.2 us
  matrix products: 45.8 us -> 0 us
  Pallas kernels: 0 us -> 35.6 us
  between operations: 14.2 us -> 0.06 us
  other arithmetic: 6.89 us -> 0 us
  starting transfers between devices: 0.01 us -> 3.55 us
    unnamed x2 -> x0, waiting for transfers between devices: 88.2 us -> none
    dot_general x4 -> x0, matrix products: 45.8 us -> none  [the longest x1 19.9 us: on_device(): jnp.dot(e_hidden, expert_down, preferred_element_type=jnp.float32)]
    pallas_call x0 -> x3, Pallas kernels: none -> 35.6 us  [the longest x1 34.3 us: branch_sums(): pl.pallas_call(branches, out_shape=jax.ShapeDtypeStruct((count, width), B...]
    all_to_all x0 -> x1, waiting for transfers between devices: none -> 12.2 us  [on_device(): lax.all_to_all(partial.reshape(devices, rows_own, width), 'ep', 0, 0, til...]
    all_to_all x0 -> x1, starting transfers between devices: none -> 3.55 us  [on_device(): lax.all_to_all(partial.reshape(devices, rows_own, width), 'ep', 0, 0, til...]
    reduce_sum x6 -> x0, other arithmetic: 3.2 us -> none  [the longest x2 2.12 us: rms_scale(): jnp.mean(values * values, axis=-1, keepdims=True) + 1e-06]
where the time goes in v1:
time: 80.1 us; the launch traced here: 79.6 us
  Pallas kernels  35.6 us (44%)
  blocking collectives  24.2 us (30%)
  waiting for transfers between devices  12.2 us (15%)
  local copies, waits for them, and re-layouts  4.08 us (5%)
  starting transfers between devices  3.55 us (4%)
    pallas_call x1, Pallas kernels, branch_sums(): pl.pallas_call(branches, out_shape=jax.ShapeDtypeStruct((count, width), B...  34.3 us
    all_gather x1, blocking collectives, on_device(): gathered = lax.all_gather(hidden_in, 'ep', axis=0, tiled=True)  24.2 us
    all_to_all x1, waiting for transfers between devices, on_device(): lax.all_to_all(partial.reshape(devices, rows_own, width), 'ep', 0, 0, til...  12.2 us
    all_to_all x1, starting transfers between devices, on_device(): lax.all_to_all(partial.reshape(devices, rows_own, width), 'ep', 0, 0, til...  3.55 us
    unnamed x17, local copies, waits for them, and re-layouts  3.09 us
  transfers between devices with their start and end apart: 1, of which 1 were waited for; matrix products, arithmetic and copies ran while one was open for 0% of the time, Pallas kernels for 0%

profile of v1, /device:TPU:0, one launch (start us, length us, event | category | flops | bytes accessed | tf_op | source)
XLA Modules:
  0.0 79.6 jit_solution(2438036470249609213)
XLA Ops:
  0.0 0.0 copy-start
  0.0 0.8 copy-done
  0.8 0.0 copy-start.7
  0.8 0.7 copy-done.7
  1.5 0.2 shard_map.109.hidden_ref
  1.7 24.2 %all-gather = bf16[16,2,6144]{2,1,0:T(2,128)(2,1)S(1)} all-gather(bf16[1,2,6144]{2,1,0:T(2,128)(2,1)S(1)} %bitcast.7), channel_id=1, replica_groups=mesh['groups'=2,'ep'=16] {'ep'}, dimensions={0}, use_global_device_ids=true | all-gather | bytes 417792 | tf_op jit(solution)/shard_map/all_gather | solution.py:245
  25.9 0.1 reshape.13.rows_ref
  26.0 0.0 copy-start.2
  26.0 0.7 copy-done.2
  26.7 0.0 copy-start.4
  26.7 0.7 copy-done.4
  27.4 0.0 copy-start.1
  27.4 0.0 copy-start.3
  27.4 0.0 copy-start.5
  27.4 0.0 copy-start.6
  27.4 34.3 %shard_map.110 = bf16[32,6144]{1,0:T(8,128)(2,1)S(1)} custom-call(s32[1]{0:T(128)} %bitcast.1.expert_ref, bf16[32,6144]{1,0:T(8,128)(2,1)S(1)} %reshape.13.rows_ref, s32[12,32]{1,0:T(8,128)S(1)} %bitcast.8, s32[12,32]{1,0:T(8,128)S(1)} %bitcast.10, bf16[6144,2048]{1,0:T(8,128)(2,1)} %eg_ref.1, bf16[6144,2048]{1,0:T(8,128)(2,1)} %eu_ref.1, ...), custom_call_target="tpu_custom_call" | custom-call | flops 3321888768 | bytes 103809024 | tf_op jit(solution)/shard_map/pallas_call | solution.py:169
  61.7 1.0 %reshape.10 = bf16[16,2,6144]{2,1,0:T(2,128)(2,1)} reshape(bf16[32,6144]{1,0:T(8,128)(2,1)S(1)} %shard_map.110) | data formatting | bytes 786432 | tf_op jit(solution)/shard_map/reshape | solution.py:259
  62.7 3.6 %all-to-all-start = ((bf16[16,2,6144]{2,1,0:T(2,128)(2,1)}), bf16[16,2,6144]{2,1,0:T(2,128)(2,1)S(1)}, u32[]{:S(2)}, u32[]{:S(2)}) async-start(bf16[16,2,6144]{2,1,0:T(2,128)(2,1)} %reshape.10), calls=%async_computation | async-start | bytes 786432 | tf_op jit(solution)/shard_map/all_to_all | solution.py:258
  66.3 12.2 %all-to-all-done.received_ref = bf16[16,2,6144]{2,1,0:T(2,128)(2,1)S(1)} async-done(((bf16[16,2,6144]{2,1,0:T(2,128)(2,1)}), bf16[16,2,6144]{2,1,0:T(2,128)(2,1)S(1)}, u32[]{:S(2)}, u32[]{:S(2)}) %all-to-all-start) | async-done | bytes 393248 | tf_op jit(solution)/shard_map/all_to_all | solution.py:258
  78.4 0.0 copy-done.1
  78.4 0.0 copy-done.3
  78.4 0.0 copy-done.5
  78.4 0.0 copy-done.6
  78.5 1.2 %shard_map.111 = f32[2,6144]{1,0:T(2,128)} custom-call(s32[1]{0:T(128)} %bitcast.first_ref, bf16[16,2,6144]{2,1,0:T(2,128)(2,1)S(1)} %all-to-all-done.received_ref, bf16[2,6144]{1,0:T(2,128)(2,1)S(1)} %shard_map.109.hidden_ref, s32[12,32]{1,0:T(8,128)S(1)} %bitcast.9, s32[12,32]{1,0:T(8,128)S(1)} %bitcast.11, f32[2,6144]{1,0:T(2,128)S(1)} %copy-done.1, ...), custom_call_target="tpu_custom_call" | custom-call | tf_op jit(solution)/shard_map/pallas_call | solution.py:217
Async XLA Ops:
  0.0 0.8 %copy-start = (f32[2,6144]{1,0:T(2,128)S(1)}, f32[2,6144]{1,0:T(2,128)}, u32[]{:S(2)}) copy-start(f32[2,6144]{1,0:T(2,128)} %inputs_ref.3) | copy-start | bytes 147460
  0.8 0.7 copy-start.7
  26.0 0.7 copy-start.2
  26.7 0.7 copy-start.4
  27.4 51.0 %copy-start.1 = (f32[2,6144]{1,0:T(2,128)S(1)}, f32[2,6144]{1,0:T(2,128)}, u32[]{:S(2)}) copy-start(f32[2,6144]{1,0:T(2,128)} %inputs_ref.3) | copy-start | bytes 147460
  27.4 51.0 %copy-start.3 = (s32[32,12]{0,1:T(8,128)S(1)}, s32[32,12]{0,1:T(8,128)}, u32[]{:S(2)}) copy-start(s32[32,12]{0,1:T(8,128)} %param.19) | copy-start | bytes 4612
  27.4 51.0 %copy-start.5 = (s32[32,12]{0,1:T(8,128)S(1)}, s32[32,12]{0,1:T(8,128)}, u32[]{:S(2)}) copy-start(s32[32,12]{0,1:T(8,128)} %param.20) | copy-start | bytes 4612
  27.4 51.0 %copy-start.6 = (f32[6144]{0:T(1024)S(1)}, f32[6144]{0:T(1024)}, u32[]{:S(2)}) copy-start(f32[6144]{0:T(1024)} %param.21) | copy-start | bytes 73732
  62.7 15.7 %all-to-all-start = ((bf16[16,2,6144]{2,1,0:T(2,128)(2,1)}), bf16[16,2,6144]{2,1,0:T(2,128)(2,1)S(1)}, u32[]{:S(2)}, u32[]{:S(2)}) async-start(bf16[16,2,6144]{2,1,0:T(2,128)(2,1)} %reshape.10), calls=%async_computation | async-start | bytes 786432 | tf_op jit(solution)/shard_map/all_to_all | solution.py:258

commit v2 on v1

--- a/solution.py
+++ b/solution.py
@@ -8,6 +8,7 @@
 from jax.sharding import PartitionSpec as P
 
 EXPERTS = 16
+FLOPS_PER_BYTE = 1000
 BF16, F32 = jnp.bfloat16, jnp.float32
 VMEM = pl.BlockSpec(memory_space=pltpu.VMEM)
 SMEM = pl.BlockSpec(memory_space=pltpu.SMEM)
@@ -35,13 +36,16 @@
     out_ref[...] = (rms_scale(inputs_ref[...]) * gain_ref[...]).astype(out_ref.dtype)
 
 
-def normed(inputs, gain):
+def normed(inputs, gain, ahead):
     return pl.pallas_call(
         norm_rows,
         out_shape=jax.ShapeDtypeStruct(inputs.shape, BF16),
         in_specs=[VMEM, VMEM],
         out_specs=VMEM,
-        compiler_params=pltpu.CompilerParams(vmem_limit_bytes=8 << 20),
+        compiler_params=pltpu.CompilerParams(vmem_limit_bytes=1 << 20),
+        cost_estimate=pl.CostEstimate(
+            flops=FLOPS_PER_BYTE * ahead, bytes_accessed=inputs.nbytes, transcendentals=0
+        ),
     )(inputs, gain.reshape(1, -1))
 
 
@@ -107,31 +111,31 @@
     dd_ref,
     ed_ref,
     out_ref,
-    eg_slots,
     eu_slots,
     dg_slots,
     du_slots,
     dd_slots,
-    ed_slots,
     eg_sum,
     eu_sum,
     dg_sum,
     du_sum,
+    rows_flat,
     first_sems,
     second_sems,
 ):
-    width = rows_ref.shape[1]
-    kb, cb = eg_slots.shape[1], dd_slots.shape[2]
+    count, width = rows_flat.shape
+    rows_flat[...] = rows_ref[...].reshape(count, width)
+    kb, cb = eu_slots.shape[1], dd_slots.shape[2]
     first = Stream(
-        [eg_ref, eu_ref, dg_ref, du_ref],
-        [eg_slots, eu_slots, dg_slots, du_slots],
+        [eu_ref, dg_ref, du_ref],
+        [eu_slots, dg_slots, du_slots],
         first_sems,
         width // kb,
         lambda ref, step: ref.at[aligned(step, kb), :],
     )
     second = Stream(
-        [dd_ref, ed_ref],
-        [dd_slots, ed_slots],
+        [dd_ref],
+        [dd_slots],
         second_sems,
         width // cb,
         lambda ref, step: ref.at[:, aligned(step, cb)],
@@ -143,8 +147,9 @@
         total[...] = jnp.zeros_like(total)
 
     def gate_up(step, blocks):
-        part = rows_ref[:, aligned(step, kb)]
-        for total, block in zip(sums, blocks):
+        at = aligned(step, kb)
+        part = rows_flat[:, at]
+        for total, block in zip(sums, [eg_ref.at[at, :]] + blocks):
             total[...] += jnp.dot(part, block[...], preferred_element_type=F32)
 
     first.run(gate_up)
@@ -153,45 +158,52 @@
     weight = column_weights(expert_ref[0], ids_ref, route_ref)
 
     def down(step, blocks):
+        at = aligned(step, cb)
         dense = jnp.dot(d_hidden, blocks[0][...], preferred_element_type=F32)
-        routed = jnp.dot(e_hidden, blocks[1][...], preferred_element_type=F32)
-        out_ref[:, aligned(step, cb)] = (dense + routed * weight).astype(out_ref.dtype)
+        routed = jnp.dot(e_hidden, ed_ref[:, at], preferred_element_type=F32)
+        out_ref[:, at] = (dense + routed * weight).astype(out_ref.dtype)
 
     second.run(down)
 
 
 def branch_sums(expert, rows, ids, route, e_gate, e_up, d_gate, d_up, d_down, e_down):
-    count, width = rows.shape
+    count, width = rows.shape[0] * rows.shape[1], rows.shape[2]
     dense, units = d_gate.shape[1], e_gate.shape[1]
     kb, cb = block_of(width, 256), block_of(width, 512)
     depth = 3
-    weights = [in_hbm(a) for a in (e_gate, e_up, d_gate, d_up, d_down, e_down)]
+    weights = [
+        in_vmem(e_gate),
+        in_hbm(e_up),
+        in_hbm(d_gate),
+        in_hbm(d_up),
+        in_hbm(d_down),
+        in_vmem(e_down),
+    ]
     return pl.pallas_call(
         branches,
         out_shape=jax.ShapeDtypeStruct((count, width), BF16),
-        in_specs=[SMEM, VMEM, VMEM, VMEM] + [HBM] * 6,
+        in_specs=[SMEM, VMEM, VMEM, VMEM, VMEM, HBM, HBM, HBM, HBM, VMEM],
         out_specs=VMEM,
         scratch_shapes=[
-            pltpu.VMEM((depth, kb, units), BF16),
             pltpu.VMEM((depth, kb, units), BF16),
             pltpu.VMEM((depth, kb, dense), BF16),
             pltpu.VMEM((depth, kb, dense), BF16),
             pltpu.VMEM((depth, dense, cb), BF16),
-            pltpu.VMEM((depth, units, cb), BF16),
             pltpu.VMEM((count, units), F32),
             pltpu.VMEM((count, units), F32),
             pltpu.VMEM((count, dense), F32),
             pltpu.VMEM((count, dense), F32),
-            pltpu.SemaphoreType.DMA((4, depth)),
-            pltpu.SemaphoreType.DMA((2, depth)),
+            pltpu.VMEM((count, width), BF16),
+            pltpu.SemaphoreType.DMA((3, depth)),
+            pltpu.SemaphoreType.DMA((1, depth)),
         ],
-        compiler_params=pltpu.CompilerParams(vmem_limit_bytes=40 << 20),
+        compiler_params=pltpu.CompilerParams(vmem_limit_bytes=11 << 20),
         cost_estimate=pl.CostEstimate(
             flops=6 * count * width * (dense + units),
             bytes_accessed=6 * width * (dense + units),
             transcendentals=count * (dense + units),
         ),
-    )(expert, rows, ids, route, *weights)
+    )(expert, in_vmem(rows), ids, route, *weights)
 
 
 def join(
@@ -241,8 +253,8 @@
     my_index = lax.axis_index("ep")
     expert = my_index // (devices // EXPERTS)
     ids, route = expert_ids.T, route_weights.T
-    hidden_in = normed(inputs, norm_gain)
-    gathered = lax.all_gather(hidden_in, "ep", axis=0, tiled=True)
+    hidden_in = normed(inputs, norm_gain, expert_gate.nbytes + expert_down.nbytes)
+    gathered = lax.all_gather(hidden_in, "ep", axis=0, tiled=False)
     partial = branch_sums(
         expert[None],
         gathered,

time: 80.1 us -> 71.9 us (0.90)
  Pallas kernels: 35.6 us -> 27.9 us
    pallas_call x1, Pallas kernels: 34.3 us -> 26.5 us  [branch_sums(): pl.pallas_call(branches, out_shape=jax.ShapeDtypeStruct((count, width), B...]
    unnamed x17 -> x16, local copies, waits for them, and re-layouts: 3.09 us -> 1.56 us
    reshape x1, local copies, waits for them, and re-layouts: 1 us -> 1.99 us  [on_device(): partial.reshape(devices, rows_own, width)]
where the time goes in v2:
time: 71.9 us; the launch traced here: 71.5 us
  Pallas kernels  27.9 us (39%)
  blocking collectives  24.3 us (34%)
  waiting for transfers between devices  12.2 us (17%)
  local copies, waits for them, and re-layouts  3.55 us (5%)
  starting transfers between devices  3.55 us (5%)
    pallas_call x1, Pallas kernels, branch_sums(): pl.pallas_call(branches, out_shape=jax.ShapeDtypeStruct((count, width), B...  26.5 us
    all_gather x1, blocking collectives, on_device(): gathered = lax.all_gather(hidden_in, 'ep', axis=0, tiled=False)  24.3 us
    all_to_all x1, waiting for transfers between devices, on_device(): lax.all_to_all(partial.reshape(devices, rows_own, width), 'ep', 0, 0, til...  12.2 us
    all_to_all x1, starting transfers between devices, on_device(): lax.all_to_all(partial.reshape(devices, rows_own, width), 'ep', 0, 0, til...  3.55 us
    reshape x1, local copies, waits for them, and re-layouts, on_device(): partial.reshape(devices, rows_own, width)  1.99 us
    unnamed x16, local copies, waits for them, and re-layouts  1.56 us
  transfers between devices with their start and end apart: 1, of which 1 were waited for; matrix products, arithmetic and copies ran while one was open for 0% of the time, Pallas kernels for 0%

profile of v2, /device:TPU:0, one launch (start us, length us, event | category | flops | bytes accessed | tf_op | source)
XLA Modules:
  0.0 71.5 jit_solution(3354433151208081587)
XLA Ops:
  0.0 0.0 copy-start.2
  0.0 0.8 %copy-done.2 = f32[2,6144]{1,0:T(2,128)S(1)} copy-done((f32[2,6144]{1,0:T(2,128)S(1)}, f32[2,6144]{1,0:T(2,128)}, u32[]{:S(2)}) %copy-start.2) | copy-done | bytes 49176
  0.8 0.0 copy-start.7
  0.8 0.7 %copy-done.7 = f32[6144]{0:T(1024)S(1)} copy-done((f32[6144]{0:T(1024)S(1)}, f32[6144]{0:T(1024)}, u32[]{:S(2)}) %copy-start.7) | copy-done | bytes 24600
  1.5 0.0 copy-start
  1.5 0.0 copy-start.1
  1.5 0.2 shard_map.109.hidden_ref
  1.7 24.3 %all-gather.1.rows_ref = bf16[16,2,6144]{2,1,0:T(2,128)(2,1)S(1)} all-gather(bf16[1,2,6144]{2,1,0:T(2,128)(2,1)S(1)} %bitcast.7), channel_id=2, replica_groups=mesh['groups'=2,'ep'=16] {'ep'}, dimensions={0}, use_global_device_ids=true | all-gather | bytes 417792 | tf_op jit(solution)/shard_map/all_gather | solution.py:257
  26.0 0.0 copy-done
  26.0 0.0 copy-done.1
  26.0 0.0 copy-start.3
  26.0 0.0 copy-start.4
  26.0 0.0 copy-start.5
  26.0 0.0 copy-start.6
  26.0 26.5 %shard_map.110 = bf16[32,6144]{1,0:T(8,128)(2,1)} custom-call(s32[1]{0:T(128)} %bitcast.1.expert_ref, bf16[16,2,6144]{2,1,0:T(2,128)(2,1)S(1)} %all-gather.1.rows_ref, s32[12,32]{1,0:T(8,128)} %bitcast.8, s32[12,32]{1,0:T(8,128)} %bitcast.10, bf16[6144,2048]{1,0:T(8,128)(2,1)S(1)} %copy-done, bf16[6144,2048]{1,0:T(8,128)(2,1)} %eu_ref.1, ...), custom_call_target="tpu_custom_call" | custom-call | flops 3321888768 | bytes 103809024 | tf_op jit(solution)/shard_map/pallas_call | solution.py:182
  52.6 2.0 %reshape.10 = bf16[16,2,6144]{2,1,0:T(2,128)(2,1)} reshape(bf16[32,6144]{1,0:T(8,128)(2,1)} %shard_map.110) | data formatting | bytes 786432 | tf_op jit(solution)/shard_map/reshape | solution.py:271
  54.6 3.6 %all-to-all-start = ((bf16[16,2,6144]{2,1,0:T(2,128)(2,1)}), bf16[16,2,6144]{2,1,0:T(2,128)(2,1)S(1)}, u32[]{:S(2)}, u32[]{:S(2)}) async-start(bf16[16,2,6144]{2,1,0:T(2,128)(2,1)} %reshape.10), calls=%async_computation | async-start | bytes 786432 | tf_op jit(solution)/shard_map/all_to_all | solution.py:270
  58.1 12.2 %all-to-all-done.received_ref = bf16[16,2,6144]{2,1,0:T(2,128)(2,1)S(1)} async-done(((bf16[16,2,6144]{2,1,0:T(2,128)(2,1)}), bf16[16,2,6144]{2,1,0:T(2,128)(2,1)S(1)}, u32[]{:S(2)}, u32[]{:S(2)}) %all-to-all-start) | async-done | bytes 393248 | tf_op jit(solution)/shard_map/all_to_all | solution.py:270
  70.3 0.0 copy-done.3
  70.3 0.0 copy-done.4
  70.3 0.0 copy-done.5
  70.3 0.0 copy-done.6
  70.3 1.2 %shard_map.111 = f32[2,6144]{1,0:T(2,128)} custom-call(s32[1]{0:T(128)} %bitcast.first_ref, bf16[16,2,6144]{2,1,0:T(2,128)(2,1)S(1)} %all-to-all-done.received_ref, bf16[2,6144]{1,0:T(2,128)(2,1)S(1)} %shard_map.109.hidden_ref, s32[12,32]{1,0:T(8,128)S(1)} %bitcast.9, s32[12,32]{1,0:T(8,128)S(1)} %bitcast.11, f32[2,6144]{1,0:T(2,128)S(1)} %copy-done.3, ...), custom_call_target="tpu_custom_call" | custom-call | tf_op jit(solution)/shard_map/pallas_call | solution.py:229
Async XLA Ops:
  0.0 0.8 %copy-start.2 = (f32[2,6144]{1,0:T(2,128)S(1)}, f32[2,6144]{1,0:T(2,128)}, u32[]{:S(2)}) copy-start(f32[2,6144]{1,0:T(2,128)} %inputs_ref.3) | copy-start | bytes 147460
  0.8 0.7 %copy-start.7 = (f32[6144]{0:T(1024)S(1)}, f32[6144]{0:T(1024)}, u32[]{:S(2)}) copy-start(f32[6144]{0:T(1024)} %param.12) | copy-start | bytes 73732
  1.5 24.5 %copy-start = (bf16[6144,2048]{1,0:T(8,128)(2,1)S(1)}, bf16[6144,2048]{1,0:T(8,128)(2,1)}, u32[]{:S(2)}) copy-start(bf16[6144,2048]{1,0:T(8,128)(2,1)} %eg_ref.1) | copy-start | bytes 75497472
  1.5 24.5 %copy-start.1 = (bf16[2048,6144]{1,0:T(8,128)(2,1)S(1)}, bf16[2048,6144]{1,0:T(8,128)(2,1)}, u32[]{:S(2)}) copy-start(bf16[2048,6144]{1,0:T(8,128)(2,1)} %ed_ref.1) | copy-start | bytes 75497472
  26.0 44.3 %copy-start.3 = (f32[2,6144]{1,0:T(2,128)S(1)}, f32[2,6144]{1,0:T(2,128)}, u32[]{:S(2)}) copy-start(f32[2,6144]{1,0:T(2,128)} %inputs_ref.3) | copy-start | bytes 147460
  26.0 44.3 %copy-start.4 = (s32[32,12]{0,1:T(8,128)S(1)}, s32[32,12]{0,1:T(8,128)}, u32[]{:S(2)}) copy-start(s32[32,12]{0,1:T(8,128)} %param.19) | copy-start | bytes 4612
  26.0 44.3 %copy-start.5 = (s32[32,12]{0,1:T(8,128)S(1)}, s32[32,12]{0,1:T(8,128)}, u32[]{:S(2)}) copy-start(s32[32,12]{0,1:T(8,128)} %param.20) | copy-start | bytes 4612
  26.0 44.3 %copy-start.6 = (f32[6144]{0:T(1024)S(1)}, f32[6144]{0:T(1024)}, u32[]{:S(2)}) copy-start(f32[6144]{0:T(1024)} %param.21) | copy-start | bytes 73732
  54.6 15.7 %all-to-all-start = ((bf16[16,2,6144]{2,1,0:T(2,128)(2,1)}), bf16[16,2,6144]{2,1,0:T(2,128)(2,1)S(1)}, u32[]{:S(2)}, u32[]{:S(2)}) async-start(bf16[16,2,6144]{2,1,0:T(2,128)(2,1)} %reshape.10), calls=%async_computation | async-start | bytes 786432 | tf_op jit(solution)/shard_map/all_to_all | solution.py:270

commit v3 on v2

--- a/solution.py
+++ b/solution.py
@@ -46,7 +46,22 @@
         cost_estimate=pl.CostEstimate(
             flops=FLOPS_PER_BYTE * ahead, bytes_accessed=inputs.nbytes, transcendentals=0
         ),
-    )(inputs, gain.reshape(1, -1))
+    )(in_hbm(inputs), in_hbm(gain.reshape(1, -1)))
+
+
+def gathered_rows(own, axis):
+    devices = lax.axis_size(axis)
+    assert devices & (devices - 1) == 0
+    rows, places = own[None], [0]
+    stages = [[1 << b] for b in range(2, devices.bit_length() - 1)] + [[1, 2]]
+    for bits in stages:
+        among = [0]
+        for bit in bits:
+            among = among + [k | bit for k in among]
+        groups = [[i | k for k in among] for i in range(devices) if not i & among[-1]]
+        rows = lax.all_gather(rows, axis, axis=0, tiled=True, axis_index_groups=groups)
+        places = [p | k for k in among for p in places]
+    return rows, places
 
 
 class Stream:
@@ -86,21 +101,27 @@
     return pl.ds(pl.multiple_of(step * size, size), size)
 
 
-def column_weights(expert, ids_ref, route_ref):
+def column_weights(expert, places, ids_ref, route_ref):
     count = ids_ref.shape[1]
+    rows = count // len(places)
     across = jnp.sum(
         jnp.where(ids_ref[...] == expert, route_ref[...].astype(F32) / 1024.0, 0.0),
         axis=0,
         keepdims=True,
     )
-    same = lax.broadcasted_iota(jnp.int32, (count, count), 0) == lax.broadcasted_iota(
-        jnp.int32, (count, count), 1
-    )
+    at = lax.broadcasted_iota(jnp.int32, (count, 1), 0)
+    row = jnp.zeros_like(at)
+    for k, place in enumerate(places):
+        shift = (place - k) * rows
+        row = jnp.where((at >= k * rows) & (at < (k + 1) * rows), at + shift, row)
+    same = row == lax.broadcasted_iota(jnp.int32, (count, count), 1)
     return jnp.sum(jnp.where(same, across, 0.0), axis=1, keepdims=True)
 
 
 def branches(
-    expert_ref,
+    places,
+    slices,
+    me_ref,
     rows_ref,
     ids_ref,
     route_ref,
@@ -124,7 +145,7 @@
     second_sems,
 ):
     count, width = rows_flat.shape
-    rows_flat[...] = rows_ref[...].reshape(count, width)
+    rows = count // len(places)
     kb, cb = eu_slots.shape[1], dd_slots.shape[2]
     first = Stream(
         [eu_ref, dg_ref, du_ref],
@@ -142,6 +163,7 @@
     )
     first.fill()
     second.fill()
+    rows_flat[...] = rows_ref[...].reshape(count, width)
     sums = [eg_sum, eu_sum, dg_sum, du_sum]
     for total in sums:
         total[...] = jnp.zeros_like(total)
@@ -155,22 +177,25 @@
     first.run(gate_up)
     e_hidden = (jax.nn.silu(eg_sum[...]) * eu_sum[...]).astype(BF16)
     d_hidden = (jax.nn.silu(dg_sum[...]) * du_sum[...]).astype(BF16)
-    weight = column_weights(expert_ref[0], ids_ref, route_ref)
+    weight = column_weights(me_ref[0] // slices, places, ids_ref, route_ref)
 
     def down(step, blocks):
         at = aligned(step, cb)
         dense = jnp.dot(d_hidden, blocks[0][...], preferred_element_type=F32)
         routed = jnp.dot(e_hidden, ed_ref[:, at], preferred_element_type=F32)
-        out_ref[:, at] = (dense + routed * weight).astype(out_ref.dtype)
+        part = (dense + routed * weight).astype(out_ref.dtype).reshape(len(places), rows, cb)
+        for k, place in enumerate(places):
+            out_ref[place, :, at] = part[k]
 
     second.run(down)
 
 
-def branch_sums(expert, rows, ids, route, e_gate, e_up, d_gate, d_up, d_down, e_down):
-    count, width = rows.shape[0] * rows.shape[1], rows.shape[2]
+def branch_sums(me, gathered, places, ids, route, e_gate, e_up, d_gate, d_up, d_down, e_down):
+    devices, rows, width = gathered.shape
+    count = devices * rows
     dense, units = d_gate.shape[1], e_gate.shape[1]
-    kb, cb = block_of(width, 256), block_of(width, 512)
-    depth = 3
+    kb, cb = block_of(width, 512), block_of(width, 512)
+    depth = 2
     weights = [
         in_vmem(e_gate),
         in_hbm(e_up),
@@ -180,9 +205,9 @@
         in_vmem(e_down),
     ]
     return pl.pallas_call(
-        branches,
-        out_shape=jax.ShapeDtypeStruct((count, width), BF16),
-        in_specs=[SMEM, VMEM, VMEM, VMEM, VMEM, HBM, HBM, HBM, HBM, VMEM],
+        functools.partial(branches, places, devices // EXPERTS),
+        out_shape=jax.ShapeDtypeStruct((devices, rows, width), BF16),
+        in_specs=[SMEM] + [VMEM] * 4 + [HBM] * 4 + [VMEM],
         out_specs=VMEM,
         scratch_shapes=[
             pltpu.VMEM((depth, kb, units), BF16),
@@ -203,7 +228,7 @@
             bytes_accessed=6 * width * (dense + units),
             transcendentals=count * (dense + units),
         ),
-    )(expert, in_vmem(rows), ids, route, *weights)
+    )(me, in_vmem(gathered), ids, route, *weights)
 
 
 def join(
@@ -248,16 +273,15 @@
     route_weights,
     out_gain,
 ):
-    devices = lax.axis_size("ep")
-    rows_own, width = inputs.shape
+    rows_own = inputs.shape[0]
     my_index = lax.axis_index("ep")
-    expert = my_index // (devices // EXPERTS)
     ids, route = expert_ids.T, route_weights.T
     hidden_in = normed(inputs, norm_gain, expert_gate.nbytes + expert_down.nbytes)
-    gathered = lax.all_gather(hidden_in, "ep", axis=0, tiled=False)
+    gathered, places = gathered_rows(hidden_in, "ep")
     partial = branch_sums(
-        expert[None],
+        my_index[None],
         gathered,
+        places,
         ids,
         route,
         expert_gate,
@@ -267,9 +291,7 @@
         dense_down,
         expert_down,
     )
-    received = lax.all_to_all(
-        partial.reshape(devices, rows_own, width), "ep", 0, 0, tiled=True
-    )
+    received = lax.all_to_all(partial, "ep", 0, 0, tiled=True)
     return joined_rows(
         (my_index * rows_own)[None], received, hidden_in, ids, route, inputs, out_gain
     )

time: 71.9 us -> 69.2 us (0.962)
  blocking collectives: 24.3 us -> 18.5 us
  Pallas kernels: 27.9 us -> 32 us
  local copies, waits for them, and re-layouts: 3.55 us -> 0.03 us
  starting transfers between devices: 3.55 us -> 6.03 us
    all_gather x1 -> x3, blocking collectives: 24.3 us -> 18.5 us  [gathered_rows(): lax.all_gather(rows, axis, axis=0, tiled=True, axis_index_groups=groups)]
    pallas_call x1, Pallas kernels: 26.5 us -> 29.7 us  [branch_sums(): pl.pallas_call(functools.partial(branches, places, devices // EXPERTS), o...]
    all_to_all x1, starting transfers between devices: 3.55 us -> 6.03 us  [on_device(): received = lax.all_to_all(partial, 'ep', 0, 0, tiled=True)]
    reshape x1 -> x0, local copies, waits for them, and re-layouts: 1.99 us -> none  [on_device(): partial.reshape(devices, rows_own, width)]
    unnamed x16 -> x12, local copies, waits for them, and re-layouts: 1.56 us -> 0.03 us
    pallas_call x1, Pallas kernels: 0.16 us -> 1.11 us  [normed(): pl.pallas_call(norm_rows, out_shape=jax.ShapeDtypeStruct(inputs.shape, BF...]
where the time goes in v3:
time: 69.2 us; the launch traced here: 68.8 us
  Pallas kernels  32 us (46%)
  blocking collectives  18.5 us (27%)
  waiting for transfers between devices  12.2 us (18%)
  starting transfers between devices  6.03 us (9%)
    pallas_call x1, Pallas kernels, branch_sums(): pl.pallas_call(functools.partial(branches, places, devices // EXPERTS), o...  29.7 us
    all_gather x3, blocking collectives, gathered_rows(): lax.all_gather(rows, axis, axis=0, tiled=True, axis_index_groups=groups)  18.5 us
    all_to_all x1, waiting for transfers between devices, on_device(): received = lax.all_to_all(partial, 'ep', 0, 0, tiled=True)  12.2 us
    all_to_all x1, starting transfers between devices, on_device(): received = lax.all_to_all(partial, 'ep', 0, 0, tiled=True)  6.03 us
  transfers between devices with their start and end apart: 1, of which 1 were waited for; matrix products, arithmetic and copies ran while one was open for 0% of the time, Pallas kernels for 0%

profile of v3, /device:TPU:0, one launch (start us, length us, event | category | flops | bytes accessed | tf_op | source)
XLA Modules:
  0.0 68.8 jit_solution(4570297470115145209)
XLA Ops:
  0.0 0.0 copy-start
  0.0 0.0 copy-start.1
  0.0 1.1 %shard_map.109.hidden_ref = bf16[2,6144]{1,0:T(2,128)(2,1)S(1)} custom-call(f32[2,6144]{1,0:T(2,128)} %inputs_ref.3, f32[1,6144]{1,0:T(1,128)} %bitcast.13), custom_call_target="tpu_custom_call" | custom-call | flops 50331648000 | bytes 49152 | tf_op jit(solution)/shard_map/pallas_call | solution.py:40
  1.1 5.6 %all-gather.1 = bf16[2,2,6144]{2,1,0:T(2,128)(2,1)S(1)} all-gather(bf16[1,2,6144]{2,1,0:T(2,128)(2,1)S(1)} %bitcast.7), channel_id=2, replica_groups={{0,4},{1,5},{2,6},{3,7},{8,12},{9,13},{10,14},{11,15},{16,20},{17,21},{..., dimensions={0}, use_global_device_ids=true | all-gather | bytes 73728 | tf_op jit(solution)/shard_map/all_gather | solution.py:62
  6.7 5.9 %all_gather.10 = bf16[4,2,6144]{2,1,0:T(2,128)(2,1)S(1)} all-gather(bf16[2,2,6144]{2,1,0:T(2,128)(2,1)S(1)} %all-gather.1), channel_id=1, replica_groups={{0,8},{1,9},{2,10},{3,11},{4,12},{5,13},{6,14},{7,15},{16,24},{17,25},{..., dimensions={0}, use_global_device_ids=true | all-gather | bytes 147456 | tf_op jit(solution)/shard_map/all_gather | solution.py:62
  12.6 7.0 %all_gather.11.rows_ref = bf16[16,2,6144]{2,1,0:T(2,128)(2,1)S(1)} all-gather(bf16[4,2,6144]{2,1,0:T(2,128)(2,1)S(1)} %all_gather.10), channel_id=1, replica_groups={{0,1,2,3},{4,5,6,7},{8,9,10,11},{12,13,14,15},{16,17,18,19},{20,21,22,2..., dimensions={0}, use_global_device_ids=true | all-gather | bytes 491520 | tf_op jit(solution)/shard_map/all_gather | solution.py:62
  19.6 0.0 copy-done
  19.6 0.0 copy-done.1
  19.6 0.0 copy-start.2
  19.6 0.0 copy-start.3
  19.6 0.0 copy-start.4
  19.6 0.0 copy-start.5
  19.6 29.7 %shard_map.110 = bf16[16,2,6144]{2,1,0:T(2,128)(2,1)} custom-call(s32[1]{0:T(128)} %bitcast.1.me_ref, bf16[16,2,6144]{2,1,0:T(2,128)(2,1)S(1)} %all_gather.11.rows_ref, s32[12,32]{1,0:T(8,128)} %bitcast.8, s32[12,32]{1,0:T(8,128)} %bitcast.10, bf16[6144,2048]{1,0:T(8,128)(2,1)S(1)} %copy-done, bf16[6144,2048]{1,0:T(8,128)(2,1)} %eu_ref.1, ...), custom_call_target="tpu_custom_call" | custom-call | flops 3321888768 | bytes 103809024 | tf_op jit(solution)/shard_map/pallas_call | solution.py:207
  49.4 6.0 %all-to-all-start = ((bf16[16,2,6144]{2,1,0:T(2,128)(2,1)}), bf16[16,2,6144]{2,1,0:T(2,128)(2,1)S(1)}, u32[]{:S(2)}, u32[]{:S(2)}) async-start(bf16[16,2,6144]{2,1,0:T(2,128)(2,1)} %shard_map.110), calls=%async_computation | async-start | bytes 786432 | tf_op jit(solution)/shard_map/all_to_all | solution.py:294
  55.4 12.2 %all-to-all-done.received_ref = bf16[16,2,6144]{2,1,0:T(2,128)(2,1)S(1)} async-done(((bf16[16,2,6144]{2,1,0:T(2,128)(2,1)}), bf16[16,2,6144]{2,1,0:T(2,128)(2,1)S(1)}, u32[]{:S(2)}, u32[]{:S(2)}) %all-to-all-start) | async-done | bytes 393248 | tf_op jit(solution)/shard_map/all_to_all | solution.py:294
  67.6 0.0 copy-done.2
  67.6 0.0 copy-done.3
  67.6 0.0 copy-done.4
  67.6 0.0 copy-done.5
  67.6 1.2 %shard_map.111 = f32[2,6144]{1,0:T(2,128)} custom-call(s32[1]{0:T(128)} %bitcast.first_ref, bf16[16,2,6144]{2,1,0:T(2,128)(2,1)S(1)} %all-to-all-done.received_ref, bf16[2,6144]{1,0:T(2,128)(2,1)S(1)} %shard_map.109.hidden_ref, s32[12,32]{1,0:T(8,128)S(1)} %bitcast.9, s32[12,32]{1,0:T(8,128)S(1)} %bitcast.11, f32[2,6144]{1,0:T(2,128)S(1)} %copy-done.2, ...), custom_call_target="tpu_custom_call" | custom-call | tf_op jit(solution)/shard_map/pallas_call | solution.py:254
Async XLA Ops:
  0.0 19.6 %copy-start = (bf16[6144,2048]{1,0:T(8,128)(2,1)S(1)}, bf16[6144,2048]{1,0:T(8,128)(2,1)}, u32[]{:S(2)}) copy-start(bf16[6144,2048]{1,0:T(8,128)(2,1)} %eg_ref.1) | copy-start | bytes 75497472
  0.0 19.6 %copy-start.1 = (bf16[2048,6144]{1,0:T(8,128)(2,1)S(1)}, bf16[2048,6144]{1,0:T(8,128)(2,1)}, u32[]{:S(2)}) copy-start(bf16[2048,6144]{1,0:T(8,128)(2,1)} %ed_ref.1) | copy-start | bytes 75497472
  19.6 48.0 %copy-start.2 = (f32[2,6144]{1,0:T(2,128)S(1)}, f32[2,6144]{1,0:T(2,128)}, u32[]{:S(2)}) copy-start(f32[2,6144]{1,0:T(2,128)} %inputs_ref.3) | copy-start | bytes 147460
  19.6 48.0 %copy-start.3 = (s32[32,12]{0,1:T(8,128)S(1)}, s32[32,12]{0,1:T(8,128)}, u32[]{:S(2)}) copy-start(s32[32,12]{0,1:T(8,128)} %param.19) | copy-start | bytes 4612
  19.6 48.0 %copy-start.4 = (s32[32,12]{0,1:T(8,128)S(1)}, s32[32,12]{0,1:T(8,128)}, u32[]{:S(2)}) copy-start(s32[32,12]{0,1:T(8,128)} %param.20) | copy-start | bytes 4612
  19.6 48.0 %copy-start.5 = (f32[6144]{0:T(1024)S(1)}, f32[6144]{0:T(1024)}, u32[]{:S(2)}) copy-start(f32[6144]{0:T(1024)} %param.21) | copy-start | bytes 73732
  49.4 18.2 %all-to-all-start = ((bf16[16,2,6144]{2,1,0:T(2,128)(2,1)}), bf16[16,2,6144]{2,1,0:T(2,128)(2,1)S(1)}, u32[]{:S(2)}, u32[]{:S(2)}) async-start(bf16[16,2,6144]{2,1,0:T(2,128)(2,1)} %shard_map.110), calls=%async_computation | async-start | bytes 786432 | tf_op jit(solution)/shard_map/all_to_all | solution.py:294

commit v4 on v3

--- a/solution.py
+++ b/solution.py
@@ -9,6 +9,7 @@
 
 EXPERTS = 16
 FLOPS_PER_BYTE = 1000
+VMEM_GRANT = 14 << 20
 BF16, F32 = jnp.bfloat16, jnp.float32
 VMEM = pl.BlockSpec(memory_space=pltpu.VMEM)
 SMEM = pl.BlockSpec(memory_space=pltpu.SMEM)
@@ -62,39 +63,6 @@
         rows = lax.all_gather(rows, axis, axis=0, tiled=True, axis_index_groups=groups)
         places = [p | k for k in among for p in places]
     return rows, places
-
-
-class Stream:
-    def __init__(self, sources, slots, sems, steps, at):
-        self.sources, self.slots, self.sems, self.steps, self.at = sources, slots, sems, steps, at
-        self.depth = slots[0].shape[0]
-
-    def copies(self, step, slot):
-        return [
-            pltpu.make_async_copy(self.at(source, step), buffer.at[slot], self.sems.at[i, slot])
-            for i, (source, buffer) in enumerate(zip(self.sources, self.slots))
-        ]
-
-    def fill(self):
-        for step in range(min(self.depth, self.steps)):
-            for copy in self.copies(step, step):
-                copy.start()
-
-    def run(self, use):
-        def body(step, _):
-            slot = lax.rem(step, self.depth)
-            for copy in self.copies(step, slot):
-                copy.wait()
-            use(step, [buffer.at[slot] for buffer in self.slots])
-
-            @pl.when(step + self.depth < self.steps)
-            def _():
-                for copy in self.copies(step + self.depth, slot):
-                    copy.start()
-
-            return 0
-
-        lax.fori_loop(0, self.steps, body, 0)
 
 
 def aligned(step, size):
@@ -132,70 +100,132 @@
     dd_ref,
     ed_ref,
     out_ref,
-    eu_slots,
-    dg_slots,
-    du_slots,
-    dd_slots,
+    slots,
+    halves,
+    rows_flat,
     eg_sum,
     eu_sum,
     dg_sum,
     du_sum,
-    rows_flat,
-    first_sems,
-    second_sems,
+    e_hidden,
+    d_hidden,
+    routed,
+    sems,
 ):
     count, width = rows_flat.shape
     rows = count // len(places)
-    kb, cb = eu_slots.shape[1], dd_slots.shape[2]
-    first = Stream(
-        [eu_ref, dg_ref, du_ref],
-        [eu_slots, dg_slots, du_slots],
-        first_sems,
-        width // kb,
-        lambda ref, step: ref.at[aligned(step, kb), :],
-    )
-    second = Stream(
-        [dd_ref],
-        [dd_slots],
-        second_sems,
-        width // cb,
-        lambda ref, step: ref.at[:, aligned(step, cb)],
-    )
-    first.fill()
-    second.fill()
+    depth, high, units = slots.shape
+    dense = dg_ref.shape[1]
+    steps, parts = width // high, -(-dense // high)
+    tall, blocks = dense // parts, width // units
+    ends = (steps, 2 * steps, 2 * steps + parts * blocks)
+
+    def half(k, slot):
+        if dense % 128:
+            return halves.at[k, slot]
+        return slots.at[slot, :, pl.ds(k * dense, dense)]
+
+    def pair(ref, at, buffer, sem):
+        return pltpu.make_async_copy(ref.at[at], buffer, sem)
+
+    def up_copies(item, slot):
+        return [pair(eu_ref, (aligned(item, high), slice(None)), slots.at[slot], sems.at[0, slot])]
+
+    def branch_copies(item, slot):
+        at = (aligned(item - ends[0], high), slice(None))
+        return [
+            pair(ref, at, half(k, slot), sems.at[k, slot]) for k, ref in enumerate((dg_ref, du_ref))
+        ]
+
+    def last_copies(item, slot):
+        item = item - ends[1]
+        at = (aligned(lax.rem(item, parts), tall), aligned(lax.div(item, parts), units))
+        return [pair(dd_ref, at, slots.at[slot, pl.ds(0, tall), :], sems.at[0, slot])]
+
+    def bring(item):
+        slot = lax.rem(item, depth)
+        firsts = (0, *ends[:2])
+        for first, end, copies in zip(firsts, ends, (up_copies, branch_copies, last_copies)):
+
+            @pl.when((item >= first) & (item < end))
+            def _():
+                for copy in copies(item, slot):
+                    copy.start()
+
+    def wait(copies, item):
+        slot = lax.rem(item, depth)
+        for copy in copies(item, slot):
+            copy.wait()
+        return slot
+
+    for item in range(depth):
+        bring(jnp.int32(item))
     rows_flat[...] = rows_ref[...].reshape(count, width)
-    sums = [eg_sum, eu_sum, dg_sum, du_sum]
-    for total in sums:
+    for total in (eg_sum, eu_sum, dg_sum, du_sum):
         total[...] = jnp.zeros_like(total)
 
-    def gate_up(step, blocks):
-        at = aligned(step, kb)
-        part = rows_flat[:, at]
-        for total, block in zip(sums, [eg_ref.at[at, :]] + blocks):
-            total[...] += jnp.dot(part, block[...], preferred_element_type=F32)
-
-    first.run(gate_up)
-    e_hidden = (jax.nn.silu(eg_sum[...]) * eu_sum[...]).astype(BF16)
-    d_hidden = (jax.nn.silu(dg_sum[...]) * du_sum[...]).astype(BF16)
+    def add(total, at, block):
+        total[...] += jnp.dot(rows_flat[:, at], block[...], preferred_element_type=F32)
+
+    widest = block_of(width, 4 * high)
+
+    def expert_gate(step, _):
+        at = aligned(step, widest)
+        add(eg_sum, at, eg_ref.at[at, :])
+        return 0
+
+    def expert_up(step, _):
+        slot = wait(up_copies, step)
+        add(eu_sum, aligned(step, high), slots.at[slot])
+        bring(step + depth)
+        return 0
+
+    lax.fori_loop(0, width // widest, expert_gate, 0)
+    lax.fori_loop(0, steps, expert_up, 0)
+    e_hidden[...] = (jax.nn.silu(eg_sum[...]) * eu_sum[...]).astype(BF16)
     weight = column_weights(me_ref[0] // slices, places, ids_ref, route_ref)
 
-    def down(step, blocks):
-        at = aligned(step, cb)
-        dense = jnp.dot(d_hidden, blocks[0][...], preferred_element_type=F32)
-        routed = jnp.dot(e_hidden, ed_ref[:, at], preferred_element_type=F32)
-        part = (dense + routed * weight).astype(out_ref.dtype).reshape(len(places), rows, cb)
+    def expert_down(step, _):
+        at, item = aligned(step, high), step + ends[0]
+        slot = wait(branch_copies, item)
+        add(dg_sum, at, half(0, slot))
+        add(du_sum, at, half(1, slot))
+        routed[:, at] = weight * jnp.dot(
+            e_hidden[...], ed_ref[:, at], preferred_element_type=F32
+        )
+        bring(item + depth)
+        return 0
+
+    lax.fori_loop(0, steps, expert_down, 0)
+    d_hidden[...] = (jax.nn.silu(dg_sum[...]) * du_sum[...]).astype(BF16)
+
+    def dense_down(step, _):
+        at, item = aligned(step, units), step * parts + ends[1]
+        part = routed[:, at]
+        for k in range(parts):
+            slot = wait(last_copies, item + k)
+            part += jnp.dot(
+                d_hidden[:, k * tall : (k + 1) * tall],
+                slots[slot, :tall, :],
+                preferred_element_type=F32,
+            )
+            bring(item + k + depth)
+        part = part.astype(out_ref.dtype).reshape(len(places), rows, units)
         for k, place in enumerate(places):
             out_ref[place, :, at] = part[k]
-
-    second.run(down)
+        return 0
+
+    lax.fori_loop(0, blocks, dense_down, 0)
 
 
 def branch_sums(me, gathered, places, ids, route, e_gate, e_up, d_gate, d_up, d_down, e_down):
     devices, rows, width = gathered.shape
     count = devices * rows
     dense, units = d_gate.shape[1], e_gate.shape[1]
-    kb, cb = block_of(width, 512), block_of(width, 512)
-    depth = 2
+    high, depth = block_of(width, 512), 5
+    assert width % units == 0 and dense % -(-dense // high) == 0
+    assert dense % 128 or 2 * dense <= units
+    halves = (2, depth, high, dense) if dense % 128 else (2, 1, 16, 128)
     weights = [
         in_vmem(e_gate),
         in_hbm(e_up),
@@ -210,19 +240,19 @@
         in_specs=[SMEM] + [VMEM] * 4 + [HBM] * 4 + [VMEM],
         out_specs=VMEM,
         scratch_shapes=[
-            pltpu.VMEM((depth, kb, units), BF16),
-            pltpu.VMEM((depth, kb, dense), BF16),
-            pltpu.VMEM((depth, kb, dense), BF16),
-            pltpu.VMEM((depth, dense, cb), BF16),
+            pltpu.VMEM((depth, high, units), BF16),
+            pltpu.VMEM(halves, BF16),
+            pltpu.VMEM((count, width), BF16),
             pltpu.VMEM((count, units), F32),
             pltpu.VMEM((count, units), F32),
             pltpu.VMEM((count, dense), F32),
             pltpu.VMEM((count, dense), F32),
-            pltpu.VMEM((count, width), BF16),
-            pltpu.SemaphoreType.DMA((3, depth)),
-            pltpu.SemaphoreType.DMA((1, depth)),
+            pltpu.VMEM((count, units), BF16),
+            pltpu.VMEM((count, dense), BF16),
+            pltpu.VMEM((count, width), F32),
+            pltpu.SemaphoreType.DMA((2, depth)),
         ],
-        compiler_params=pltpu.CompilerParams(vmem_limit_bytes=11 << 20),
+        compiler_params=pltpu.CompilerParams(vmem_limit_bytes=VMEM_GRANT),
         cost_estimate=pl.CostEstimate(
             flops=6 * count * width * (dense + units),
             bytes_accessed=6 * width * (dense + units),

time: 69.2 us -> 63.3 us (0.915)
  Pallas kernels: 32 us -> 26.3 us
    pallas_call x1, Pallas kernels: 29.7 us -> 24 us  [branch_sums(): pl.pallas_call(functools.partial(branches, places, devices // EXPERTS), o...]
where the time goes in v4:
time: 63.3 us; the launch traced here: 63.1 us
  Pallas kernels  26.3 us (42%)
  blocking collectives  18.5 us (29%)
  waiting for transfers between devices  12.2 us (19%)
  starting transfers between devices  6.02 us (10%)
    pallas_call x1, Pallas kernels, branch_sums(): pl.pallas_call(functools.partial(branches, places, devices // EXPERTS), o...  24 us
    all_gather x3, blocking collectives, gathered_rows(): lax.all_gather(rows, axis, axis=0, tiled=True, axis_index_groups=groups)  18.5 us
    all_to_all x1, waiting for transfers between devices, on_device(): received = lax.all_to_all(partial, 'ep', 0, 0, tiled=True)  12.2 us
    all_to_all x1, starting transfers between devices, on_device(): received = lax.all_to_all(partial, 'ep', 0, 0, tiled=True)  6.02 us
  transfers between devices with their start and end apart: 1, of which 1 were waited for; matrix products, arithmetic and copies ran while one was open for 0% of the time, Pallas kernels for 0%

profile of v4, /device:TPU:0, one launch (start us, length us, event | category | flops | bytes accessed | tf_op | source)
XLA Modules:
  0.0 63.1 jit_solution(1472350660640182599)
XLA Ops:
  0.0 0.0 copy-start
  0.0 0.0 copy-start.1
  0.0 1.1 %shard_map.109.hidden_ref = bf16[2,6144]{1,0:T(2,128)(2,1)S(1)} custom-call(f32[2,6144]{1,0:T(2,128)} %inputs_ref.3, f32[1,6144]{1,0:T(1,128)} %bitcast.13), custom_call_target="tpu_custom_call" | custom-call | flops 50331648000 | bytes 49152 | tf_op jit(solution)/shard_map/pallas_call | solution.py:41
  1.1 5.6 %all-gather.1 = bf16[2,2,6144]{2,1,0:T(2,128)(2,1)S(1)} all-gather(bf16[1,2,6144]{2,1,0:T(2,128)(2,1)S(1)} %bitcast.7), channel_id=2, replica_groups={{0,4},{1,5},{2,6},{3,7},{8,12},{9,13},{10,14},{11,15},{16,20},{17,21},{..., dimensions={0}, use_global_device_ids=true | all-gather | bytes 73728 | tf_op jit(solution)/shard_map/all_gather | solution.py:63
  6.7 5.9 %all_gather.10 = bf16[4,2,6144]{2,1,0:T(2,128)(2,1)S(1)} all-gather(bf16[2,2,6144]{2,1,0:T(2,128)(2,1)S(1)} %all-gather.1), channel_id=1, replica_groups={{0,8},{1,9},{2,10},{3,11},{4,12},{5,13},{6,14},{7,15},{16,24},{17,25},{..., dimensions={0}, use_global_device_ids=true | all-gather | bytes 147456 | tf_op jit(solution)/shard_map/all_gather | solution.py:63
  12.6 7.0 %all_gather.11.rows_ref = bf16[16,2,6144]{2,1,0:T(2,128)(2,1)S(1)} all-gather(bf16[4,2,6144]{2,1,0:T(2,128)(2,1)S(1)} %all_gather.10), channel_id=1, replica_groups={{0,1,2,3},{4,5,6,7},{8,9,10,11},{12,13,14,15},{16,17,18,19},{20,21,22,2..., dimensions={0}, use_global_device_ids=true | all-gather | bytes 491520 | tf_op jit(solution)/shard_map/all_gather | solution.py:63
  19.6 0.0 copy-done
  19.6 0.0 copy-done.1
  19.6 0.0 copy-start.2
  19.6 0.0 copy-start.3
  19.6 0.0 copy-start.4
  19.6 0.0 copy-start.5
  19.6 24.0 %shard_map.110 = bf16[16,2,6144]{2,1,0:T(2,128)(2,1)} custom-call(s32[1]{0:T(128)} %bitcast.1.me_ref, bf16[16,2,6144]{2,1,0:T(2,128)(2,1)S(1)} %all_gather.11.rows_ref, s32[12,32]{1,0:T(8,128)} %bitcast.8, s32[12,32]{1,0:T(8,128)} %bitcast.10, bf16[6144,2048]{1,0:T(8,128)(2,1)S(1)} %copy-done, bf16[6144,2048]{1,0:T(8,128)(2,1)} %eu_ref.1, ...), custom_call_target="tpu_custom_call" | custom-call | flops 3321888768 | bytes 103809024 | tf_op jit(solution)/shard_map/pallas_call | solution.py:237
  43.6 6.0 %all-to-all-start = ((bf16[16,2,6144]{2,1,0:T(2,128)(2,1)}), bf16[16,2,6144]{2,1,0:T(2,128)(2,1)S(1)}, u32[]{:S(2)}, u32[]{:S(2)}) async-start(bf16[16,2,6144]{2,1,0:T(2,128)(2,1)} %shard_map.110), calls=%async_computation | async-start | bytes 786432 | tf_op jit(solution)/shard_map/all_to_all | solution.py:324
  49.7 12.2 %all-to-all-done.received_ref = bf16[16,2,6144]{2,1,0:T(2,128)(2,1)S(1)} async-done(((bf16[16,2,6144]{2,1,0:T(2,128)(2,1)}), bf16[16,2,6144]{2,1,0:T(2,128)(2,1)S(1)}, u32[]{:S(2)}, u32[]{:S(2)}) %all-to-all-start) | async-done | bytes 393248 | tf_op jit(solution)/shard_map/all_to_all | solution.py:324
  61.9 0.0 copy-done.2
  61.9 0.0 copy-done.3
  61.9 0.0 copy-done.4
  61.9 0.0 copy-done.5
  61.9 1.2 %shard_map.111 = f32[2,6144]{1,0:T(2,128)} custom-call(s32[1]{0:T(128)} %bitcast.first_ref, bf16[16,2,6144]{2,1,0:T(2,128)(2,1)S(1)} %all-to-all-done.received_ref, bf16[2,6144]{1,0:T(2,128)(2,1)S(1)} %shard_map.109.hidden_ref, s32[12,32]{1,0:T(8,128)S(1)} %bitcast.9, s32[12,32]{1,0:T(8,128)S(1)} %bitcast.11, f32[2,6144]{1,0:T(2,128)S(1)} %copy-done.2, ...), custom_call_target="tpu_custom_call" | custom-call | tf_op jit(solution)/shard_map/pallas_call | solution.py:284
Async XLA Ops:
  0.0 19.6 %copy-start = (bf16[6144,2048]{1,0:T(8,128)(2,1)S(1)}, bf16[6144,2048]{1,0:T(8,128)(2,1)}, u32[]{:S(2)}) copy-start(bf16[6144,2048]{1,0:T(8,128)(2,1)} %eg_ref.1) | copy-start | bytes 75497472
  0.0 19.6 %copy-start.1 = (bf16[2048,6144]{1,0:T(8,128)(2,1)S(1)}, bf16[2048,6144]{1,0:T(8,128)(2,1)}, u32[]{:S(2)}) copy-start(bf16[2048,6144]{1,0:T(8,128)(2,1)} %ed_ref.1) | copy-start | bytes 75497472
  19.6 42.3 %copy-start.2 = (f32[2,6144]{1,0:T(2,128)S(1)}, f32[2,6144]{1,0:T(2,128)}, u32[]{:S(2)}) copy-start(f32[2,6144]{1,0:T(2,128)} %inputs_ref.3) | copy-start | bytes 147460
  19.6 42.3 %copy-start.3 = (s32[32,12]{0,1:T(8,128)S(1)}, s32[32,12]{0,1:T(8,128)}, u32[]{:S(2)}) copy-start(s32[32,12]{0,1:T(8,128)} %param.19) | copy-start | bytes 4612
  19.6 42.3 %copy-start.4 = (s32[32,12]{0,1:T(8,128)S(1)}, s32[32,12]{0,1:T(8,128)}, u32[]{:S(2)}) copy-start(s32[32,12]{0,1:T(8,128)} %param.20) | copy-start | bytes 4612
  19.6 42.3 %copy-start.5 = (f32[6144]{0:T(1024)S(1)}, f32[6144]{0:T(1024)}, u32[]{:S(2)}) copy-start(f32[6144]{0:T(1024)} %param.21) | copy-start | bytes 73732
  43.6 18.2 %all-to-all-start = ((bf16[16,2,6144]{2,1,0:T(2,128)(2,1)}), bf16[16,2,6144]{2,1,0:T(2,128)(2,1)S(1)}, u32[]{:S(2)}, u32[]{:S(2)}) async-start(bf16[16,2,6144]{2,1,0:T(2,128)(2,1)} %shard_map.110), calls=%async_computation | async-start | bytes 786432 | tf_op jit(solution)/shard_map/all_to_all | solution.py:324

commit v5 on v4

--- a/solution.py
+++ b/solution.py
@@ -9,7 +9,8 @@
 
 EXPERTS = 16
 FLOPS_PER_BYTE = 1000
-VMEM_GRANT = 14 << 20
+TILE = 256
+VMEM_GRANT = 15 << 20
 BF16, F32 = jnp.bfloat16, jnp.float32
 VMEM = pl.BlockSpec(memory_space=pltpu.VMEM)
 SMEM = pl.BlockSpec(memory_space=pltpu.SMEM)
@@ -84,6 +85,94 @@
         row = jnp.where((at >= k * rows) & (at < (k + 1) * rows), at + shift, row)
     same = row == lax.broadcasted_iota(jnp.int32, (count, count), 1)
     return jnp.sum(jnp.where(same, across, 0.0), axis=1, keepdims=True)
+
+
+def accumulators(rows, count):
+    return [pltpu.ACC(j % 2)((rows, TILE), F32) for j in range(count)]
+
+
+def multiply(turns, sums, lefts, right):
+    for k, left in enumerate(lefts):
+        for j, total in enumerate(sums):
+            unit = j % 2
+            stage = turns[unit] % 2
+            turns[unit] += 1
+            pltpu.matmul_push_rhs(right(k, j), stage, unit)
+            pltpu.matmul_acc_lhs(total, left, load_staged_rhs=stage)
+
+
+def tile_products(sizes, calls, refs, eg_acc, eu_acc, d_acc, routed_acc, last_acc):
+    steps, parts, blocks, ends, depth, tall = sizes
+    wait, bring, up_copies, branch_copies, last_copies, half, weights, write, flatten = calls
+    eg_ref, ed_ref, slots, rows_flat, e_hidden, d_hidden, routed = refs
+    _, high, units = slots.shape
+    deep, thin = high // TILE, len(d_acc) // 2
+
+    def tile(k):
+        return pl.ds(k * TILE, TILE)
+
+    def row_tiles(step):
+        return [rows_flat[:, aligned(step * deep + k, TILE)] for k in range(deep)]
+
+    def expert_gate(step, _):
+        def right(k, j):
+            return eg_ref[aligned(step * deep + k, TILE), tile(j)]
+
+        flatten(aligned(step, high), high)
+        multiply([0, 0], eg_acc, row_tiles(step), right)
+        return 0
+
+    def expert_up(step, _):
+        slot = wait(up_copies, step)
+        multiply([0, 0], eu_acc, row_tiles(step), lambda k, j: slots[slot, tile(k), tile(j)])
+        bring(step + depth)
+        return 0
+
+    lax.fori_loop(0, steps, expert_gate, 0)
+    lax.fori_loop(0, steps, expert_up, 0)
+    for j, (gate, upper) in enumerate(zip(eg_acc, eu_acc)):
+        hidden = jax.nn.silu(pltpu.matmul_pop(gate)) * pltpu.matmul_pop(upper)
+        e_hidden[:, j * TILE : (j + 1) * TILE] = hidden.astype(BF16)
+    weight = weights()
+
+    def expert_down(step, _):
+        item, turns = step + ends[0], [0, 0]
+
+        def right(k, j):
+            return ed_ref[tile(k), aligned(step * deep + j, TILE)]
+
+        lefts = [e_hidden[:, k * TILE : (k + 1) * TILE] for k in range(units // TILE)]
+        multiply(turns, routed_acc, lefts, right)
+        slot = wait(branch_copies, item)
+        gate, upper = half(0, slot), half(1, slot)
+
+        def dense_right(k, j):
+            return (gate if j < thin else upper)[tile(k), tile(j % thin)]
+
+        multiply(turns, d_acc, row_tiles(step), dense_right)
+        for j, total in enumerate(routed_acc):
+            routed[:, aligned(step * deep + j, TILE)] = weight * pltpu.matmul_pop(total)
+        bring(item + depth)
+        return 0
+
+    lax.fori_loop(0, steps, expert_down, 0)
+    for j in range(thin):
+        hidden = jax.nn.silu(pltpu.matmul_pop(d_acc[j])) * pltpu.matmul_pop(d_acc[thin + j])
+        d_hidden[:, j * TILE : (j + 1) * TILE] = hidden.astype(BF16)
+
+    def dense_down(step, _):
+        item, turns = step * parts + ends[1], [0, 0]
+        for k in range(parts):
+            slot = wait(last_copies, item + k)
+            left = d_hidden[:, k * TILE : (k + 1) * TILE]
+            multiply(turns, last_acc, [left], lambda _, j: slots[slot, pl.ds(0, TILE), tile(j)])
+            bring(item + k + depth)
+        for j, total in enumerate(last_acc):
+            at = aligned(step * len(last_acc) + j, TILE)
+            write(at, pltpu.matmul_pop(total) + routed[:, at])
+        return 0
+
+    lax.fori_loop(0, blocks, dense_down, 0)
 
 
 def branches(
@@ -110,13 +199,18 @@
     e_hidden,
     d_hidden,
     routed,
+    ids_here,
+    route_here,
     sems,
+    route_sems,
+    *,
+    explicit,
 ):
     count, width = rows_flat.shape
     rows = count // len(places)
     depth, high, units = slots.shape
     dense = dg_ref.shape[1]
-    steps, parts = width // high, -(-dense // high)
+    steps, parts = width // high, dense // TILE if explicit else -(-dense // high)
     tall, blocks = dense // parts, width // units
     ends = (steps, 2 * steps, 2 * steps + parts * blocks)
 
@@ -160,7 +254,38 @@
 
     for item in range(depth):
         bring(jnp.int32(item))
-    rows_flat[...] = rows_ref[...].reshape(count, width)
+    route_copies = [
+        pltpu.make_async_copy(ids_ref, ids_here, route_sems.at[0]),
+        pltpu.make_async_copy(route_ref, route_here, route_sems.at[1]),
+    ]
+    for copy in route_copies:
+        copy.start()
+
+    def flatten(at, wide):
+        rows_flat[:, at] = rows_ref[:, :, at].reshape(count, wide)
+    def weights():
+        for copy in route_copies:
+            copy.wait()
+        return column_weights(me_ref[0] // slices, places, ids_here, route_here)
+
+    def write(at, part):
+        part = part.astype(out_ref.dtype).reshape(len(places), rows, part.shape[1])
+        for k, place in enumerate(places):
+            out_ref[place, :, at] = part[k]
+
+    on_tiles = functools.partial(
+        tile_products,
+        (steps, parts, blocks, ends, depth, tall),
+        (wait, bring, up_copies, branch_copies, last_copies, half, weights, write, flatten),
+        (eg_ref, ed_ref, slots, rows_flat, e_hidden, d_hidden, routed),
+    )
+    if explicit:
+        wide, thin = units // TILE, dense // TILE
+        pl.run_scoped(
+            on_tiles, *[accumulators(count, n) for n in (wide, wide, 2 * thin, high // TILE, wide)]
+        )
+        return
+    flatten(slice(None), width)
     for total in (eg_sum, eu_sum, dg_sum, du_sum):
         total[...] = jnp.zeros_like(total)
 
@@ -183,7 +308,7 @@
     lax.fori_loop(0, width // widest, expert_gate, 0)
     lax.fori_loop(0, steps, expert_up, 0)
     e_hidden[...] = (jax.nn.silu(eg_sum[...]) * eu_sum[...]).astype(BF16)
-    weight = column_weights(me_ref[0] // slices, places, ids_ref, route_ref)
+    weight = weights()
 
     def expert_down(step, _):
         at, item = aligned(step, high), step + ends[0]
@@ -210,9 +335,7 @@
                 preferred_element_type=F32,
             )
             bring(item + k + depth)
-        part = part.astype(out_ref.dtype).reshape(len(places), rows, units)
-        for k, place in enumerate(places):
-            out_ref[place, :, at] = part[k]
+        write(at, part)
         return 0
 
     lax.fori_loop(0, blocks, dense_down, 0)
@@ -222,9 +345,11 @@
     devices, rows, width = gathered.shape
     count = devices * rows
     dense, units = d_gate.shape[1], e_gate.shape[1]
-    high, depth = block_of(width, 512), 5
+    high, depth = block_of(width, 512), 6
     assert width % units == 0 and dense % -(-dense // high) == 0
     assert dense % 128 or 2 * dense <= units
+    explicit = dense % TILE == 0 and units % TILE == 0 and high % TILE == 0 and count <= 64
+    sums = (units, units, dense, dense)
     halves = (2, depth, high, dense) if dense % 128 else (2, 1, 16, 128)
     weights = [
         in_vmem(e_gate),
@@ -235,22 +360,22 @@
         in_vmem(e_down),
     ]
     return pl.pallas_call(
-        functools.partial(branches, places, devices // EXPERTS),
+        functools.partial(branches, places, devices // EXPERTS, explicit=explicit),
         out_shape=jax.ShapeDtypeStruct((devices, rows, width), BF16),
-        in_specs=[SMEM] + [VMEM] * 4 + [HBM] * 4 + [VMEM],
+        in_specs=[SMEM, VMEM, HBM, HBM, VMEM, HBM, HBM, HBM, HBM, VMEM],
         out_specs=VMEM,
         scratch_shapes=[
             pltpu.VMEM((depth, high, units), BF16),
             pltpu.VMEM(halves, BF16),
             pltpu.VMEM((count, width), BF16),
-            pltpu.VMEM((count, units), F32),
-            pltpu.VMEM((count, units), F32),
-            pltpu.VMEM((count, dense), F32),
-            pltpu.VMEM((count, dense), F32),
+            *(pltpu.VMEM((8, 128) if explicit else (count, n), F32) for n in sums),
             pltpu.VMEM((count, units), BF16),
             pltpu.VMEM((count, dense), BF16),
             pltpu.VMEM((count, width), F32),
+            pltpu.VMEM(ids.shape, ids.dtype),
+            pltpu.VMEM(route.shape, route.dtype),
             pltpu.SemaphoreType.DMA((2, depth)),
+            pltpu.SemaphoreType.DMA((2,)),
         ],
         compiler_params=pltpu.CompilerParams(vmem_limit_bytes=VMEM_GRANT),
         cost_estimate=pl.CostEstimate(
@@ -258,7 +383,7 @@
             bytes_accessed=6 * width * (dense + units),
             transcendentals=count * (dense + units),
         ),
-    )(me, in_vmem(gathered), ids, route, *weights)
+    )(me, in_vmem(gathered), in_hbm(ids), in_hbm(route), *weights)
 
 
 def join(
@@ -341,6 +466,11 @@
         P("groups", None),
         P(),
     )
-    return jax.shard_map(
+    def program(*args):
+        with jax.sharding.use_abstract_mesh(mesh.abstract_mesh):
+            return sharded(*args)
+
+    sharded = jax.shard_map(
         on_device, mesh=mesh, in_specs=placed, out_specs=P(("groups", "ep"), None), check_vma=False
     )
+    return program

time: 63.3 us -> 60.7 us (0.959)
  Pallas kernels: 26.3 us -> 23.7 us
    pallas_call x1, Pallas kernels: 24 us -> 21.4 us  [branch_sums(): pl.pallas_call(functools.partial(branches, places, devices // EXPERTS, ex...]
where the time goes in v5:
time: 60.7 us; the launch traced here: 60.5 us
  Pallas kernels  23.7 us (39%)
  blocking collectives  18.5 us (30%)
  waiting for transfers between devices  12.2 us (20%)
  starting transfers between devices  6.02 us (10%)
    pallas_call x1, Pallas kernels, branch_sums(): pl.pallas_call(functools.partial(branches, places, devices // EXPERTS, ex...  21.4 us
    all_gather x3, blocking collectives, gathered_rows(): lax.all_gather(rows, axis, axis=0, tiled=True, axis_index_groups=groups)  18.5 us
    all_to_all x1, waiting for transfers between devices, on_device(): received = lax.all_to_all(partial, 'ep', 0, 0, tiled=True)  12.2 us
    all_to_all x1, starting transfers between devices, on_device(): received = lax.all_to_all(partial, 'ep', 0, 0, tiled=True)  6.02 us
  transfers between devices with their start and end apart: 1, of which 1 were waited for; matrix products, arithmetic and copies ran while one was open for 0% of the time, Pallas kernels for 0%

profile of v5, /device:TPU:0, one launch (start us, length us, event | category | flops | bytes accessed | tf_op | source)
XLA Modules:
  0.0 60.5 jit_solution(15745729881280267789)
XLA Ops:
  0.0 0.0 copy-start
  0.0 0.0 copy-start.1
  0.0 1.1 %shard_map.109.hidden_ref = bf16[2,6144]{1,0:T(2,128)(2,1)S(1)} custom-call(f32[2,6144]{1,0:T(2,128)} %inputs_ref.3, f32[1,6144]{1,0:T(1,128)} %bitcast.13), custom_call_target="tpu_custom_call" | custom-call | flops 50331648000 | bytes 49152 | tf_op jit(solution)/shard_map/pallas_call | solution.py:42
  1.1 5.6 %all-gather.1 = bf16[2,2,6144]{2,1,0:T(2,128)(2,1)S(1)} all-gather(bf16[1,2,6144]{2,1,0:T(2,128)(2,1)S(1)} %bitcast.7), channel_id=2, replica_groups={{0,4},{1,5},{2,6},{3,7},{8,12},{9,13},{10,14},{11,15},{16,20},{17,21},{..., dimensions={0}, use_global_device_ids=true | all-gather | bytes 73728 | tf_op jit(solution)/shard_map/all_gather | solution.py:64
  6.7 5.9 %all_gather.10 = bf16[4,2,6144]{2,1,0:T(2,128)(2,1)S(1)} all-gather(bf16[2,2,6144]{2,1,0:T(2,128)(2,1)S(1)} %all-gather.1), channel_id=1, replica_groups={{0,8},{1,9},{2,10},{3,11},{4,12},{5,13},{6,14},{7,15},{16,24},{17,25},{..., dimensions={0}, use_global_device_ids=true | all-gather | bytes 147456 | tf_op jit(solution)/shard_map/all_gather | solution.py:64
  12.6 7.0 %all_gather.11.rows_ref = bf16[16,2,6144]{2,1,0:T(2,128)(2,1)S(1)} all-gather(bf16[4,2,6144]{2,1,0:T(2,128)(2,1)S(1)} %all_gather.10), channel_id=1, replica_groups={{0,1,2,3},{4,5,6,7},{8,9,10,11},{12,13,14,15},{16,17,18,19},{20,21,22,2..., dimensions={0}, use_global_device_ids=true | all-gather | bytes 491520 | tf_op jit(solution)/shard_map/all_gather | solution.py:64
  19.6 0.0 copy-done
  19.6 0.0 copy-done.1
  19.6 0.0 copy-start.2
  19.6 0.0 copy-start.3
  19.6 0.0 copy-start.4
  19.6 0.0 copy-start.5
  19.6 21.4 %shard_map.110 = bf16[16,2,6144]{2,1,0:T(2,128)(2,1)} custom-call(s32[1]{0:T(128)} %bitcast.1.me_ref, bf16[16,2,6144]{2,1,0:T(2,128)(2,1)S(1)} %all_gather.11.rows_ref, s32[12,32]{1,0:T(8,128)} %bitcast.8, s32[12,32]{1,0:T(8,128)} %bitcast.10, bf16[6144,2048]{1,0:T(8,128)(2,1)S(1)} %copy-done, bf16[6144,2048]{1,0:T(8,128)(2,1)} %eu_ref.1, ...), custom_call_target="tpu_custom_call" | custom-call | flops 3321888768 | bytes 103809024 | tf_op jit(solution)/shard_map/pallas_call | solution.py:362
  41.1 6.0 %all-to-all-start = ((bf16[16,2,6144]{2,1,0:T(2,128)(2,1)}), bf16[16,2,6144]{2,1,0:T(2,128)(2,1)S(1)}, u32[]{:S(2)}, u32[]{:S(2)}) async-start(bf16[16,2,6144]{2,1,0:T(2,128)(2,1)} %shard_map.110), calls=%async_computation | async-start | bytes 786432 | tf_op jit(solution)/shard_map/all_to_all | solution.py:449
  47.1 12.2 %all-to-all-done.received_ref = bf16[16,2,6144]{2,1,0:T(2,128)(2,1)S(1)} async-done(((bf16[16,2,6144]{2,1,0:T(2,128)(2,1)}), bf16[16,2,6144]{2,1,0:T(2,128)(2,1)S(1)}, u32[]{:S(2)}, u32[]{:S(2)}) %all-to-all-start) | async-done | bytes 393248 | tf_op jit(solution)/shard_map/all_to_all | solution.py:449
  59.3 0.0 copy-done.2
  59.3 0.0 copy-done.3
  59.3 0.0 copy-done.4
  59.3 0.0 copy-done.5
  59.3 1.2 %shard_map.111 = f32[2,6144]{1,0:T(2,128)} custom-call(s32[1]{0:T(128)} %bitcast.first_ref, bf16[16,2,6144]{2,1,0:T(2,128)(2,1)S(1)} %all-to-all-done.received_ref, bf16[2,6144]{1,0:T(2,128)(2,1)S(1)} %shard_map.109.hidden_ref, s32[12,32]{1,0:T(8,128)S(1)} %bitcast.9, s32[12,32]{1,0:T(8,128)S(1)} %bitcast.11, f32[2,6144]{1,0:T(2,128)S(1)} %copy-done.2, ...), custom_call_target="tpu_custom_call" | custom-call | tf_op jit(solution)/shard_map/pallas_call | solution.py:409
Async XLA Ops:
  0.0 19.6 %copy-start = (bf16[6144,2048]{1,0:T(8,128)(2,1)S(1)}, bf16[6144,2048]{1,0:T(8,128)(2,1)}, u32[]{:S(2)}) copy-start(bf16[6144,2048]{1,0:T(8,128)(2,1)} %eg_ref.1) | copy-start | bytes 75497472
  0.0 19.6 %copy-start.1 = (bf16[2048,6144]{1,0:T(8,128)(2,1)S(1)}, bf16[2048,6144]{1,0:T(8,128)(2,1)}, u32[]{:S(2)}) copy-start(bf16[2048,6144]{1,0:T(8,128)(2,1)} %ed_ref.1) | copy-start | bytes 75497472
  19.6 39.7 %copy-start.2 = (f32[2,6144]{1,0:T(2,128)S(1)}, f32[2,6144]{1,0:T(2,128)}, u32[]{:S(2)}) copy-start(f32[2,6144]{1,0:T(2,128)} %inputs_ref.3) | copy-start | bytes 147460
  19.6 39.7 %copy-start.3 = (s32[32,12]{0,1:T(8,128)S(1)}, s32[32,12]{0,1:T(8,128)}, u32[]{:S(2)}) copy-start(s32[32,12]{0,1:T(8,128)} %param.19) | copy-start | bytes 4612
  19.6 39.7 %copy-start.4 = (s32[32,12]{0,1:T(8,128)S(1)}, s32[32,12]{0,1:T(8,128)}, u32[]{:S(2)}) copy-start(s32[32,12]{0,1:T(8,128)} %param.20) | copy-start | bytes 4612
  19.6 39.7 %copy-start.5 = (f32[6144]{0:T(1024)S(1)}, f32[6144]{0:T(1024)}, u32[]{:S(2)}) copy-start(f32[6144]{0:T(1024)} %param.21) | copy-start | bytes 73732
  41.1 18.2 %all-to-all-start = ((bf16[16,2,6144]{2,1,0:T(2,128)(2,1)}), bf16[16,2,6144]{2,1,0:T(2,128)(2,1)S(1)}, u32[]{:S(2)}, u32[]{:S(2)}) async-start(bf16[16,2,6144]{2,1,0:T(2,128)(2,1)} %shard_map.110), calls=%async_computation | async-start | bytes 786432 | tf_op jit(solution)/shard_map/all_to_all | solution.py:449

commit v6 on v5

--- a/solution.py
+++ b/solution.py
@@ -13,7 +13,6 @@
 VMEM_GRANT = 15 << 20
 BF16, F32 = jnp.bfloat16, jnp.float32
 VMEM = pl.BlockSpec(memory_space=pltpu.VMEM)
-SMEM = pl.BlockSpec(memory_space=pltpu.SMEM)
 HBM = pl.BlockSpec(memory_space=pl.ANY)
 
 
@@ -103,8 +102,8 @@
 
 def tile_products(sizes, calls, refs, eg_acc, eu_acc, d_acc, routed_acc, last_acc):
     steps, parts, blocks, ends, depth, tall = sizes
-    wait, bring, up_copies, branch_copies, last_copies, half, weights, write, flatten = calls
-    eg_ref, ed_ref, slots, rows_flat, e_hidden, d_hidden, routed = refs
+    wait, bring, up_copies, branch_copies, last_copies, half, weights, write, rows_at, before, out_copy = calls
+    eg_ref, ed_ref, slots, e_hidden, d_hidden, routed = refs
     _, high, units = slots.shape
     deep, thin = high // TILE, len(d_acc) // 2
 
@@ -112,13 +111,12 @@
         return pl.ds(k * TILE, TILE)
 
     def row_tiles(step):
-        return [rows_flat[:, aligned(step * deep + k, TILE)] for k in range(deep)]
+        return [rows_at(aligned(step * deep + k, TILE), TILE) for k in range(deep)]
 
     def expert_gate(step, _):
         def right(k, j):
             return eg_ref[aligned(step * deep + k, TILE), tile(j)]
 
-        flatten(aligned(step, high), high)
         multiply([0, 0], eg_acc, row_tiles(step), right)
         return 0
 
@@ -128,7 +126,7 @@
         bring(step + depth)
         return 0
 
-    lax.fori_loop(0, steps, expert_gate, 0)
+    lax.fori_loop(0, steps, expert_gate, 0, unroll=3)
     lax.fori_loop(0, steps, expert_up, 0)
     for j, (gate, upper) in enumerate(zip(eg_acc, eu_acc)):
         hidden = jax.nn.silu(pltpu.matmul_pop(gate)) * pltpu.matmul_pop(upper)
@@ -167,9 +165,11 @@
             left = d_hidden[:, k * TILE : (k + 1) * TILE]
             multiply(turns, last_acc, [left], lambda _, j: slots[slot, pl.ds(0, TILE), tile(j)])
             bring(item + k + depth)
+        here = before(step)
         for j, total in enumerate(last_acc):
             at = aligned(step * len(last_acc) + j, TILE)
-            write(at, pltpu.matmul_pop(total) + routed[:, at])
+            write(here, tile(j), pltpu.matmul_pop(total) + routed[:, at])
+        out_copy(step).start()
         return 0
 
     lax.fori_loop(0, blocks, dense_down, 0)
@@ -178,7 +178,6 @@
 def branches(
     places,
     slices,
-    me_ref,
     rows_ref,
     ids_ref,
     route_ref,
@@ -201,13 +200,15 @@
     routed,
     ids_here,
     route_here,
+    out_here,
     sems,
     route_sems,
+    out_sems,
     *,
     explicit,
 ):
-    count, width = rows_flat.shape
-    rows = count // len(places)
+    _, rows, width = rows_ref.shape
+    count = rows * len(places)
     depth, high, units = slots.shape
     dense = dg_ref.shape[1]
     steps, parts = width // high, dense // TILE if explicit else -(-dense // high)
@@ -261,31 +262,48 @@
     for copy in route_copies:
         copy.start()
 
-    def flatten(at, wide):
-        rows_flat[:, at] = rows_ref[:, :, at].reshape(count, wide)
+    def rows_at(at, wide):
+        return rows_ref[:, :, at].reshape(count, wide)
     def weights():
         for copy in route_copies:
             copy.wait()
-        return column_weights(me_ref[0] // slices, places, ids_here, route_here)
-
-    def write(at, part):
+        return column_weights(lax.axis_index("ep") // slices, places, ids_here, route_here)
+
+    def out_copy(step):
+        at = aligned(step, units)
+        slot = lax.rem(step, 2)
+        return pltpu.make_async_copy(out_here.at[slot], out_ref.at[:, :, at], out_sems.at[slot])
+
+    def write(slot, at, part):
         part = part.astype(out_ref.dtype).reshape(len(places), rows, part.shape[1])
         for k, place in enumerate(places):
-            out_ref[place, :, at] = part[k]
+            out_here[slot, place, :, at] = part[k]
+
+    def before(step):
+        @pl.when(step >= 2)
+        def _():
+            out_copy(step - 2).wait()
+
+        return lax.rem(step, 2)
 
     on_tiles = functools.partial(
         tile_products,
         (steps, parts, blocks, ends, depth, tall),
-        (wait, bring, up_copies, branch_copies, last_copies, half, weights, write, flatten),
-        (eg_ref, ed_ref, slots, rows_flat, e_hidden, d_hidden, routed),
-    )
+        (wait, bring, up_copies, branch_copies, last_copies, half, weights, write, rows_at, before, out_copy),
+        (eg_ref, ed_ref, slots, e_hidden, d_hidden, routed),
+    )
+    def finish():
+        for step in range(max(0, blocks - 2), blocks):
+            out_copy(jnp.int32(step)).wait()
+
     if explicit:
         wide, thin = units // TILE, dense // TILE
         pl.run_scoped(
             on_tiles, *[accumulators(count, n) for n in (wide, wide, 2 * thin, high // TILE, wide)]
         )
+        finish()
         return
-    flatten(slice(None), width)
+    rows_flat[...] = rows_at(slice(None), width)
     for total in (eg_sum, eu_sum, dg_sum, du_sum):
         total[...] = jnp.zeros_like(total)
 
@@ -335,13 +353,15 @@
                 preferred_element_type=F32,
             )
             bring(item + k + depth)
-        write(at, part)
+        write(before(step), slice(None), part)
+        out_copy(step).start()
         return 0
 
     lax.fori_loop(0, blocks, dense_down, 0)
-
-
-def branch_sums(me, gathered, places, ids, route, e_gate, e_up, d_gate, d_up, d_down, e_down):
+    finish()
+
+
+def branch_sums(gathered, places, ids, route, e_gate, e_up, d_gate, d_up, d_down, e_down):
     devices, rows, width = gathered.shape
     count = devices * rows
     dense, units = d_gate.shape[1], e_gate.shape[1]
@@ -362,19 +382,21 @@
     return pl.pallas_call(
         functools.partial(branches, places, devices // EXPERTS, explicit=explicit),
         out_shape=jax.ShapeDtypeStruct((devices, rows, width), BF16),
-        in_specs=[SMEM, VMEM, HBM, HBM, VMEM, HBM, HBM, HBM, HBM, VMEM],
-        out_specs=VMEM,
+        in_specs=[VMEM, HBM, HBM, VMEM, HBM, HBM, HBM, HBM, VMEM],
+        out_specs=HBM,
         scratch_shapes=[
             pltpu.VMEM((depth, high, units), BF16),
             pltpu.VMEM(halves, BF16),
-            pltpu.VMEM((count, width), BF16),
+            pltpu.VMEM((16, 128) if explicit else (count, width), BF16),
             *(pltpu.VMEM((8, 128) if explicit else (count, n), F32) for n in sums),
             pltpu.VMEM((count, units), BF16),
             pltpu.VMEM((count, dense), BF16),
             pltpu.VMEM((count, width), F32),
             pltpu.VMEM(ids.shape, ids.dtype),
             pltpu.VMEM(route.shape, route.dtype),
+            pltpu.VMEM((2, devices, rows, units), BF16),
             pltpu.SemaphoreType.DMA((2, depth)),
+            pltpu.SemaphoreType.DMA((2,)),
             pltpu.SemaphoreType.DMA((2,)),
         ],
         compiler_params=pltpu.CompilerParams(vmem_limit_bytes=VMEM_GRANT),
@@ -383,11 +405,11 @@
             bytes_accessed=6 * width * (dense + units),
             transcendentals=count * (dense + units),
         ),
-    )(me, in_vmem(gathered), in_hbm(ids), in_hbm(route), *weights)
+    )(in_vmem(gathered), in_hbm(ids), in_hbm(route), *weights)
 
 
 def join(
-    first_ref, received_ref, hidden_ref, ids_ref, route_ref, inputs_ref, gain_ref, out_ref
+    received_ref, hidden_ref, ids_ref, route_ref, inputs_ref, gain_ref, out_ref
 ):
     rows = inputs_ref.shape[0]
     summed = jnp.sum(received_ref[...].astype(F32), axis=0)
@@ -397,22 +419,23 @@
         axis=0,
         keepdims=True,
     )
-    mine = lax.broadcasted_iota(jnp.int32, (rows, count), 1) == first_ref[
-        0
-    ] + lax.broadcasted_iota(jnp.int32, (rows, count), 0)
+    first = lax.axis_index("ep") * rows
+    mine = lax.broadcasted_iota(jnp.int32, (rows, count), 1) == first + lax.broadcasted_iota(
+        jnp.int32, (rows, count), 0
+    )
     zero_weight = jnp.sum(jnp.where(mine, across, 0.0), axis=1, keepdims=True)
     joined = summed + zero_weight * hidden_ref[...].astype(F32)
     out_ref[...] = inputs_ref[...] + rms_scale(joined) * gain_ref[...]
 
 
-def joined_rows(first, received, hidden, ids, route, inputs, gain):
+def joined_rows(received, hidden, ids, route, inputs, gain):
     return pl.pallas_call(
         join,
         out_shape=jax.ShapeDtypeStruct(inputs.shape, F32),
-        in_specs=[SMEM] + [VMEM] * 6,
+        in_specs=[VMEM] * 6,
         out_specs=VMEM,
         compiler_params=pltpu.CompilerParams(vmem_limit_bytes=24 << 20),
-    )(first, in_vmem(received), hidden, ids, route, inputs, gain.reshape(1, -1))
+    )(in_vmem(received), hidden, ids, route, inputs, gain.reshape(1, -1))
 
 
 def on_device(
@@ -428,13 +451,10 @@
     route_weights,
     out_gain,
 ):
-    rows_own = inputs.shape[0]
-    my_index = lax.axis_index("ep")
     ids, route = expert_ids.T, route_weights.T
     hidden_in = normed(inputs, norm_gain, expert_gate.nbytes + expert_down.nbytes)
     gathered, places = gathered_rows(hidden_in, "ep")
     partial = branch_sums(
-        my_index[None],
         gathered,
         places,
         ids,
@@ -448,7 +468,7 @@
     )
     received = lax.all_to_all(partial, "ep", 0, 0, tiled=True)
     return joined_rows(
-        (my_index * rows_own)[None], received, hidden_in, ids, route, inputs, out_gain
+        received, hidden_in, ids, route, inputs, out_gain
     )
 
 

time: 60.7 us -> 60.5 us (level)
  blocking collectives: 18.5 us -> 36.7 us
  waiting for transfers between devices: 12.2 us -> 0 us
  starting transfers between devices: 6.02 us -> 0 us
    all_to_all x0 -> x1, blocking collectives: none -> 18.2 us  [on_device(): received = lax.all_to_all(partial, 'ep', 0, 0, tiled=True)]
    all_to_all x1 -> x0, waiting for transfers between devices: 12.2 us -> none  [on_device(): received = lax.all_to_all(partial, 'ep', 0, 0, tiled=True)]
    all_to_all x1 -> x0, starting transfers between devices: 6.02 us -> none  [on_device(): received = lax.all_to_all(partial, 'ep', 0, 0, tiled=True)]
  transfers between devices with their start and end apart: 1 -> 0, of which waited for: 1 -> 0; matrix products, arithmetic and copies ran while one was open for 0% -> 0% of each run, Pallas kernels for 0% -> 0%
where the time goes in v6:
time: 60.5 us; the launch traced here: 60.3 us
  blocking collectives  36.7 us (61%)
  Pallas kernels  23.5 us (39%)
    pallas_call x1, Pallas kernels, branch_sums(): pl.pallas_call(functools.partial(branches, places, devices // EXPERTS, ex...  21.2 us
    all_gather x3, blocking collectives, gathered_rows(): lax.all_gather(rows, axis, axis=0, tiled=True, axis_index_groups=groups)  18.5 us
    all_to_all x1, blocking collectives, on_device(): received = lax.all_to_all(partial, 'ep', 0, 0, tiled=True)  18.2 us

profile of v6, /device:TPU:0, one launch (start us, length us, event | category | flops | bytes accessed | tf_op | source)
XLA Modules:
  0.0 60.3 jit_solution(10356256430490056153)
XLA Ops:
  0.0 0.0 copy-start
  0.0 0.0 copy-start.1
  0.0 1.1 %shard_map.109.hidden_ref = bf16[2,6144]{1,0:T(2,128)(2,1)S(1)} custom-call(f32[2,6144]{1,0:T(2,128)} %inputs_ref.3, f32[1,6144]{1,0:T(1,128)} %bitcast.11), custom_call_target="tpu_custom_call" | custom-call | flops 50331648000 | bytes 49152 | tf_op jit(solution)/shard_map/pallas_call | solution.py:41
  1.1 5.6 %all-gather.1 = bf16[2,2,6144]{2,1,0:T(2,128)(2,1)S(1)} all-gather(bf16[1,2,6144]{2,1,0:T(2,128)(2,1)S(1)} %bitcast.5), channel_id=2, replica_groups={{0,4},{1,5},{2,6},{3,7},{8,12},{9,13},{10,14},{11,15},{16,20},{17,21},{..., dimensions={0}, use_global_device_ids=true | all-gather | bytes 73728 | tf_op jit(solution)/shard_map/all_gather | solution.py:63
  6.7 5.9 %all_gather.10 = bf16[4,2,6144]{2,1,0:T(2,128)(2,1)S(1)} all-gather(bf16[2,2,6144]{2,1,0:T(2,128)(2,1)S(1)} %all-gather.1), channel_id=1, replica_groups={{0,8},{1,9},{2,10},{3,11},{4,12},{5,13},{6,14},{7,15},{16,24},{17,25},{..., dimensions={0}, use_global_device_ids=true | all-gather | bytes 147456 | tf_op jit(solution)/shard_map/all_gather | solution.py:63
  12.6 7.0 %all_gather.11.rows_ref = bf16[16,2,6144]{2,1,0:T(2,128)(2,1)S(1)} all-gather(bf16[4,2,6144]{2,1,0:T(2,128)(2,1)S(1)} %all_gather.10), channel_id=1, replica_groups={{0,1,2,3},{4,5,6,7},{8,9,10,11},{12,13,14,15},{16,17,18,19},{20,21,22,2..., dimensions={0}, use_global_device_ids=true | all-gather | bytes 491520 | tf_op jit(solution)/shard_map/all_gather | solution.py:63
  19.6 0.0 copy-done
  19.6 0.0 copy-done.1
  19.6 0.0 copy-start.2
  19.6 0.0 copy-start.3
  19.6 0.0 copy-start.4
  19.6 0.0 copy-start.5
  19.6 21.2 %shard_map.110 = bf16[16,2,6144]{2,1,0:T(2,128)(2,1)} custom-call(bf16[16,2,6144]{2,1,0:T(2,128)(2,1)S(1)} %all_gather.11.rows_ref, s32[12,32]{1,0:T(8,128)} %bitcast.6, s32[12,32]{1,0:T(8,128)} %bitcast.8, bf16[6144,2048]{1,0:T(8,128)(2,1)S(1)} %copy-done, bf16[6144,2048]{1,0:T(8,128)(2,1)} %eu_ref.1, bf16[6144,768]{1,0:T(8,128)(2,1)} %dg_ref.1, ...), custom_call_target="tpu_custom_call" | custom-call | flops 3321888768 | bytes 103809024 | tf_op jit(solution)/shard_map/pallas_call | solution.py:382
  40.9 18.2 %all_to_all.5.received_ref = bf16[16,2,6144]{2,1,0:T(2,128)(2,1)S(1)} all-to-all(bf16[16,2,6144]{2,1,0:T(2,128)(2,1)} %shard_map.110), channel_id=1, replica_groups=mesh['groups'=2,'ep'=16] {'ep'}, dimensions={0} | all-to-all | bytes 786432 | tf_op jit(solution)/shard_map/all_to_all | solution.py:469
  59.1 0.0 copy-done.2
  59.1 0.0 copy-done.3
  59.1 0.0 copy-done.4
  59.1 0.0 copy-done.5
  59.1 1.2 %shard_map.111 = f32[2,6144]{1,0:T(2,128)} custom-call(bf16[16,2,6144]{2,1,0:T(2,128)(2,1)S(1)} %all_to_all.5.received_ref, bf16[2,6144]{1,0:T(2,128)(2,1)S(1)} %shard_map.109.hidden_ref, s32[12,32]{1,0:T(8,128)S(1)} %bitcast.7, s32[12,32]{1,0:T(8,128)S(1)} %bitcast.9, f32[2,6144]{1,0:T(2,128)S(1)} %copy-done.2, f32[1,6144]{1,0:T(1,128)S(1)} %bitcast.10), custom_call_target="tpu_custom_call" | custom-call | tf_op jit(solution)/shard_map/pallas_call | solution.py:432
Async XLA Ops:
  0.0 19.6 %copy-start = (bf16[6144,2048]{1,0:T(8,128)(2,1)S(1)}, bf16[6144,2048]{1,0:T(8,128)(2,1)}, u32[]{:S(2)}) copy-start(bf16[6144,2048]{1,0:T(8,128)(2,1)} %eg_ref.1) | copy-start | bytes 75497472
  0.0 19.6 %copy-start.1 = (bf16[2048,6144]{1,0:T(8,128)(2,1)S(1)}, bf16[2048,6144]{1,0:T(8,128)(2,1)}, u32[]{:S(2)}) copy-start(bf16[2048,6144]{1,0:T(8,128)(2,1)} %ed_ref.1) | copy-start | bytes 75497472
  19.6 39.5 %copy-start.2 = (f32[2,6144]{1,0:T(2,128)S(1)}, f32[2,6144]{1,0:T(2,128)}, u32[]{:S(2)}) copy-start(f32[2,6144]{1,0:T(2,128)} %inputs_ref.3) | copy-start | bytes 147460
  19.6 39.5 %copy-start.3 = (s32[32,12]{0,1:T(8,128)S(1)}, s32[32,12]{0,1:T(8,128)}, u32[]{:S(2)}) copy-start(s32[32,12]{0,1:T(8,128)} %param.19) | copy-start | bytes 4612
  19.6 39.5 %copy-start.4 = (s32[32,12]{0,1:T(8,128)S(1)}, s32[32,12]{0,1:T(8,128)}, u32[]{:S(2)}) copy-start(s32[32,12]{0,1:T(8,128)} %param.20) | copy-start | bytes 4612
  19.6 39.5 %copy-start.5 = (f32[6144]{0:T(1024)S(1)}, f32[6144]{0:T(1024)}, u32[]{:S(2)}) copy-start(f32[6144]{0:T(1024)} %param.21) | copy-start | bytes 73732
